TPU v7x, 256 devices: a whole 4x4x8 slice. The times are simulated.
256 devices in a mesh: ctx: 64 (over y, z, core), head: 4 (over x).
Axes of the slice: x: 4, y: 4, z: 8, core: 2. Of those that a mesh axis runs over, the one named last changes fastest.
Arguments:
- queries: bfloat16 [65536, 2048], P('ctx', 'head'), may hold values from -6 to 6
- keys: bfloat16 [65536, 2048], P('ctx', 'head'), may hold values from -6 to 6
- values: bfloat16 [65536, 2048], P('ctx', 'head'), may hold values from -6 to 6
- log_decay: float32 [16, 65536], P('head', 'ctx'), may hold values from -0.8 to 0
- write_strength: float32 [16, 65536], P('head', 'ctx'), may hold values from 0 to 0.9
- level_weights: float32 [16, 12, 65536], P('head', None, 'ctx'), may hold values from 0.2 to 2
- segment: int32 [65536], P('ctx'), may hold values from 0 to 3, never falling along the last dimension, each value on 1 to 32768 neighbouring positions
- out_gate: bfloat16 [65536, 2048], P('ctx', 'head'), may hold values from -6 to 6
- norm_gain: float32 [128], replicated, may hold values from 0.1 to 1.9
- w_out: bfloat16 [2048, 2048], P('head'), may hold values from -0.125 to 0.125
Outputs:
- layer_out: bfloat16 [65536, 2048], P(('ctx', 'head'))
Inputs may be any that keep to these rules, and one draw needn't show every extreme that they name: `segment`: never falls along the sequence; each id is one contiguous run of at most 32768 tokens, and one run is exactly that long.
All inputs are finite; a program needn't handle non-finite values.
Results may differ from a plain program's by a relative error of at most 0.024.
Values may be sent and summed in bfloat16 or wider, within the bound.
A program may use at most 128 MiB of HBM per device.

v0:
```python
import jax
import jax.numpy as jnp
from jax import lax
from jax.experimental import pallas as pl
from jax.experimental.pallas import tpu as pltpu
from jax.sharding import PartitionSpec as P

BLOCK = 128
BLOCKS = 8
TOKENS_HERE = 1024
HEADS_HERE = 4
WIDTH = 128
LEVELS = 12
EPSILON = 1e-06
FAR = -1e4
MESSAGE_ROWS = 144

F32 = jnp.float32
BF16 = jnp.bfloat16


def dot(left, right):
    return jnp.dot(left, right, preferred_element_type=F32)


def dot_rows(left, right):
    return lax.dot_general(left, right, (((1,), (1,)), ((), ())), preferred_element_type=F32)


def dot_columns(left, right):
    return lax.dot_general(left, right, (((0,), (0,)), ((), ())), preferred_element_type=F32)


def split3(value):
    first = value.astype(BF16)
    rest = value - first.astype(F32)
    second = rest.astype(BF16)
    third = (rest - second.astype(F32)).astype(BF16)
    return first, second, third


def rows_of(block):
    return slice(block * BLOCK, (block + 1) * BLOCK)


def weight_column(level):
    return level if level < 8 else level + 4


def prepare_masks(seg_ref, far_ref, pair_ref):
    row = lax.broadcasted_iota(jnp.int32, (BLOCK, BLOCK), 0)
    col = lax.broadcasted_iota(jnp.int32, (BLOCK, BLOCK), 1)
    segs = seg_ref[...].astype(F32)
    padded = jnp.concatenate([segs, jnp.zeros((BLOCK - BLOCKS, BLOCK), F32)], axis=0)
    seg_cols = padded.T
    for block in range(BLOCKS):
        same = seg_cols[:, block : block + 1] == segs[block : block + 1, :]
        far_ref[block] = jnp.where(same & (row >= col), 0.0, FAR)
    for step in range(7):
        size = 1 << step
        chosen = (row // size == col // size + 1) & (row // size % 2 == 1)
        pair_ref[step] = jnp.where(chosen, 1.0, 0.0).astype(BF16)


def unit_rows(rows, ones):
    wide = rows.astype(F32)
    total = dot((wide * wide).astype(BF16), ones)
    return (wide * lax.rsqrt(total + EPSILON)).astype(BF16)


def head_terms(q, k, v, decay, strength, level_weights, segs, far_ref, pair_ref):
    row = lax.broadcasted_iota(jnp.int32, (BLOCK, BLOCK), 0)
    col = lax.broadcasted_iota(jnp.int32, (BLOCK, BLOCK), 1)
    every = range(BLOCKS)
    ones = jnp.ones((BLOCK, BLOCK), BF16)
    upto = jnp.where(row <= col, 1.0, 0.0).astype(BF16)
    summed = sum(dot(part, upto) for part in split3(decay))
    last_sum = jnp.broadcast_to(summed[:, BLOCK - 1 :], (BLOCKS, BLOCK))
    last_seg = jnp.broadcast_to(segs[:, BLOCK - 1 :], (BLOCKS, BLOCK))
    first_seg = jnp.broadcast_to(segs[:, :1], (BLOCKS, BLOCK))
    before = jnp.concatenate([first_seg[:1], last_seg[:-1]], axis=0)
    opening = jnp.exp(summed) * (segs == before).astype(F32)
    closing = jnp.exp(last_sum - summed) * (segs == last_seg).astype(F32)
    keeps = jnp.exp(last_sum) * (last_seg == before).astype(F32)
    stacked = jnp.concatenate(
        [summed, strength, opening, strength * opening, closing, jnp.zeros((BLOCK - 40, BLOCK), F32)], axis=0
    )
    cols = stacked.T
    wcols = jnp.concatenate(level_weights, axis=0).T

    def column(kind, block):
        return cols[:, kind * 8 + block : kind * 8 + block + 1]

    def weight(level, block):
        at = block * 16 + weight_column(level)
        return wcols[:, at : at + 1]

    qn = unit_rows(q, ones)
    kn = unit_rows(k, ones)
    grams = [
        dot_rows(jnp.concatenate([kn[rows_of(b)], qn[rows_of(b)]], axis=0), kn[rows_of(b)]) for b in every
    ]
    fading = [jnp.exp(column(0, b) - summed[b : b + 1, :] + far_ref[b]) for b in every]
    lower = [(column(1, b) * fading[b] * grams[b][:BLOCK]).astype(BF16) for b in every]
    scores = [(fading[b] * grams[b][BLOCK:]).astype(BF16) for b in every]
    eye = jnp.where(row == col, 1.0, 0.0).astype(BF16)
    inverse = [eye - lower[b] * pair_ref[0] for b in every]
    for step in range(1, 7):
        mask = pair_ref[step]
        half = [dot(inverse[b], lower[b] * mask).astype(BF16) for b in every]
        inverse = [inverse[b] - dot(half[b], inverse[b]).astype(BF16) for b in every]
    right = [
        jnp.concatenate(
            [
                (column(1, b) * v[rows_of(b)].astype(F32)).astype(BF16),
                (column(3, b) * kn[rows_of(b)].astype(F32)).astype(BF16),
            ],
            axis=1,
        )
        for b in every
    ]
    solved = [dot(inverse[b], right[b]).astype(BF16) for b in every]
    read = [dot(scores[b], solved[b]) for b in every]
    out = [weight(0, b) * read[b][:, :WIDTH] for b in every]
    reads = [column(2, b) * qn[rows_of(b)].astype(F32) - read[b][:, WIDTH:] for b in every]
    ended = [(column(4, b) * kn[rows_of(b)].astype(F32)).astype(BF16) for b in every]
    joined = [dot_columns(ended[b], solved[b]) for b in every]
    fresh = [joined[b][:, :WIDTH] for b in every]
    erase = [joined[b][:, WIDTH:] for b in every]
    keep = [keeps[b : b + 1] for b in every]
    for level in range(1, 4):
        span = 1 << (level - 1)
        fresh2, erase2, keep2 = [], [], []
        for pair in range(len(fresh) // 2):
            e, o = 2 * pair, 2 * pair + 1
            later = [b for b in every if b // span == o]
            stack = jnp.concatenate([reads[b] for b in later] + [erase[o]], axis=0).astype(BF16)
            both = dot(stack, jnp.concatenate([fresh[e], erase[e]], axis=1).astype(BF16))
            for at, b in enumerate(later):
                part = both[at * BLOCK : (at + 1) * BLOCK]
                out[b] = out[b] + weight(level, b) * part[:, :WIDTH]
                reads[b] = keep[e] * reads[b] - part[:, WIDTH:]
            part = both[len(later) * BLOCK :]
            fresh2.append(keep[o] * fresh[e] - part[:, :WIDTH] + fresh[o])
            erase2.append(keep[o] * erase[e] + keep[e] * erase[o] - part[:, WIDTH:])
            keep2.append(keep[e] * keep[o])
        fresh, erase, keep = fresh2, erase2, keep2
    return out, reads, fresh[0], erase[0], keep[0]


def local_kernel(q_ref, k_ref, v_ref, decay_ref, strength_ref, weights_ref, seg_ref, out_ref, read_ref, message_ref, far_ref, pair_ref, spread_ref):
    head = pl.program_id(0)

    @pl.when(head == 0)
    def _():
        prepare_masks(seg_ref, far_ref, pair_ref)
        for source, at in ((decay_ref, 0), (strength_ref, 1)):
            for each in range(HEADS_HERE):
                for b in range(BLOCKS):
                    spread_ref[at, each, b : b + 1, :] = source[each : each + 1, rows_of(b)]

    weights = [
        part
        for b in range(BLOCKS)
        for part in (weights_ref[0, 0:8, rows_of(b)], weights_ref[0, 4:12, rows_of(b)])
    ]
    out, reads, fresh, erase, keep = head_terms(
        q_ref[...],
        k_ref[...],
        v_ref[...],
        spread_ref[0, head],
        spread_ref[1, head],
        weights,
        seg_ref[...].astype(F32),
        far_ref,
        pair_ref,
    )
    for b in range(BLOCKS):
        out_ref[rows_of(b), :] = out[b]
        read_ref[rows_of(b), :] = reads[b].astype(BF16)
    message_ref[0, :BLOCK, :WIDTH] = fresh.astype(BF16)
    message_ref[0, :BLOCK, WIDTH:] = erase.astype(BF16)
    wide = jnp.concatenate([keep, keep], axis=1)
    first, second, third = split3(wide)
    message_ref[0, BLOCK:, :] = jnp.concatenate(
        [first.astype(F32), second.astype(F32), third.astype(F32), jnp.zeros((13, 2 * WIDTH), F32)], axis=0
    ).astype(BF16)


def local_terms(queries, keys, values, decay, strength, weights, segs):
    tall = pl.BlockSpec((TOKENS_HERE, WIDTH), lambda h: (0, h))
    whole = pl.BlockSpec((HEADS_HERE, TOKENS_HERE), lambda h: (0, 0))
    return pl.pallas_call(
        local_kernel,
        grid=(HEADS_HERE,),
        in_specs=[
            tall,
            tall,
            tall,
            whole,
            whole,
            pl.BlockSpec((1, LEVELS, TOKENS_HERE), lambda h: (h, 0, 0)),
            pl.BlockSpec((BLOCKS, BLOCK), lambda h: (0, 0)),
        ],
        out_specs=[tall, tall, pl.BlockSpec((1, MESSAGE_ROWS, 2 * WIDTH), lambda h: (h, 0, 0))],
        out_shape=[
            jax.ShapeDtypeStruct((TOKENS_HERE, HEADS_HERE * WIDTH), F32),
            jax.ShapeDtypeStruct((TOKENS_HERE, HEADS_HERE * WIDTH), BF16),
            jax.ShapeDtypeStruct((HEADS_HERE, MESSAGE_ROWS, 2 * WIDTH), BF16),
        ],
        scratch_shapes=[
            pltpu.VMEM((BLOCKS, BLOCK, BLOCK), F32),
            pltpu.VMEM((7, BLOCK, BLOCK), BF16),
            pltpu.VMEM((2, HEADS_HERE, BLOCKS, BLOCK), F32),
        ],
        compiler_params=pltpu.CompilerParams(vmem_limit_bytes=48 << 20),
        cost_estimate=pl.CostEstimate(flops=20_000_000_000, bytes_accessed=8_000_000, transcendentals=0),
    )(queries, keys, values, decay, strength, weights, segs)


def finish_block(out, read, states, columns, gate, gain, ones):
    wide = read.astype(F32)
    lhs = jnp.concatenate([(column * wide).astype(BF16) for column in columns], axis=1)
    total = out + dot(lhs, states)
    mean = dot((total * total).astype(BF16), ones) * (1.0 / WIDTH)
    gate = gate.astype(F32)
    silu = gate / (1.0 + jnp.exp(-gate))
    return (total * lax.rsqrt(mean + EPSILON) * gain * silu).astype(BF16)


def finish_kernel(out_ref, read_ref, states_ref, weights_ref, gate_ref, gain_ref, normed_ref):
    ones = jnp.ones((WIDTH, WIDTH), BF16)
    weights = jnp.concatenate([weights_ref[0, 4:12, rows_of(b)] for b in range(BLOCKS)], axis=0)
    weights = jnp.concatenate([weights, jnp.zeros((BLOCK - 8 * BLOCKS, BLOCK), F32)], axis=0).T
    for b in range(BLOCKS):
        columns = [weights[:, b * 8 + level : b * 8 + level + 1] for level in range(6)]
        normed_ref[rows_of(b), :] = finish_block(
            out_ref[rows_of(b), :],
            read_ref[rows_of(b), :],
            states_ref[0],
            columns,
            gate_ref[rows_of(b), :],
            gain_ref[...],
            ones,
        )


def finish(out, read, states, weights, gate, gain):
    tall = pl.BlockSpec((TOKENS_HERE, WIDTH), lambda h: (0, h))
    return pl.pallas_call(
        finish_kernel,
        grid=(HEADS_HERE,),
        in_specs=[
            tall,
            tall,
            pl.BlockSpec((1, 6 * WIDTH, WIDTH), lambda h: (h, 0, 0)),
            pl.BlockSpec((1, LEVELS, TOKENS_HERE), lambda h: (h, 0, 0)),
            tall,
            pl.BlockSpec((1, WIDTH), lambda h: (0, 0)),
        ],
        out_specs=tall,
        out_shape=jax.ShapeDtypeStruct((TOKENS_HERE, HEADS_HERE * WIDTH), BF16),
        compiler_params=pltpu.CompilerParams(vmem_limit_bytes=48 << 20),
        cost_estimate=pl.CostEstimate(flops=2_000_000_000, bytes_accessed=6_000_000, transcendentals=0),
    )(out, read, states, weights, gate, gain)


def partner(value, bit):
    return lax.ppermute(value, "ctx", [(i, i ^ 1 << bit) for i in range(lax.axis_size("ctx"))])


def unpack(message):
    keep = jnp.sum(message[:, BLOCK : BLOCK + 3, :1].astype(F32), axis=1, keepdims=True)
    body = message[:, :BLOCK].astype(F32)
    return keep, body


def pack(keep, body):
    wide = jnp.broadcast_to(keep, (HEADS_HERE, 1, 2 * WIDTH))
    zeros = jnp.zeros((HEADS_HERE, 13, 2 * WIDTH), BF16)
    return jnp.concatenate([body.astype(BF16), *split3(wide), zeros], axis=1)


def compose(later, earlier):
    keep_l, body_l = later
    keep_e, body_e = earlier
    erase = body_l[:, :, WIDTH:].astype(BF16)
    moved = jnp.einsum("hij,hjk->hik", erase, body_e.astype(BF16), preferred_element_type=F32)
    carried = jnp.concatenate([body_l[:, :, :WIDTH], keep_e * body_l[:, :, WIDTH:]], axis=2)
    return keep_l * keep_e, keep_l * body_e + carried - moved


def scan_levels(message, flag):
    position = lax.axis_index("ctx")
    keep, body = unpack(message)
    scale = jnp.where(lax.broadcasted_iota(jnp.int32, body.shape, 2) < WIDTH, 1.0, flag)
    total = keep * flag, body * scale
    prefix = jnp.ones_like(keep), jnp.zeros_like(body)
    states = []
    for bit in range(6):
        upper = position >> bit & 1 == 1
        other = unpack(partner(pack(*total), bit))
        moved = compose((prefix[0], prefix[1].at[:, :, :WIDTH].set(0.0)), other)
        states.append(jnp.where(upper, flag * moved[1][:, :, :WIDTH], 0.0).astype(BF16))
        prefix = jnp.where(upper, moved[0], prefix[0]), jnp.where(upper, moved[1], prefix[1])
        later = tuple(jnp.where(upper, a, b) for a, b in zip(total, other))
        earlier = tuple(jnp.where(upper, b, a) for a, b in zip(total, other))
        total = compose(later, earlier)
    return jnp.concatenate(states, axis=1)


def shards(queries, keys, values, log_decay, write_strength, level_weights, segment, out_gate, norm_gain, w_out):
    count = lax.axis_size("ctx")
    before = lax.ppermute(segment[-1:] + 1, "ctx", [(i, i + 1) for i in range(count - 1)]) - 1
    flag = (before[0] == segment[0]).astype(F32)
    whole = lax.all_gather(w_out, "head", axis=0, tiled=True)
    out, read, message = local_terms(
        queries, keys, values, log_decay, write_strength, level_weights, segment.reshape(BLOCKS, BLOCK)
    )
    states = scan_levels(message, flag)
    normed = finish(out, read, states, level_weights, out_gate, norm_gain.reshape(1, WIDTH))
    gathered = lax.all_to_all(normed, "head", split_axis=0, concat_axis=1, tiled=True)
    return jnp.dot(gathered, whole, preferred_element_type=F32).astype(BF16)


def solution(mesh):
    placed = (
        P("ctx", "head"),
        P("ctx", "head"),
        P("ctx", "head"),
        P("head", "ctx"),
        P("head", "ctx"),
        P("head", None, "ctx"),
        P("ctx"),
        P("ctx", "head"),
        P(),
        P("head", None),
    )
    return jax.shard_map(
        shards, mesh=mesh, in_specs=placed, out_specs=P(("ctx", "head"), None), check_vma=False
    )
```

profile of v0, /device:TPU:8, one launch (start us, length us, event | category | flops | bytes accessed | tf_op | source)
XLA Modules:
  0.0 157.7 jit_solution(12028177927553970194)
XLA Ops:
  6.5 1.4 fusion.108
  8.5 2.7 %collective-permute-start = (s32[1]{0:T(128)}, s32[1]{0:T(128)}, u32[]{:S(2)}, u32[]{:S(2)}) collective-permute-start(s32[1]{0:T(128)} %add.61), channel_id=1, source_target_pairs={{0,4},{4,8},{8,12},{12,16},{16,20},{20,24},{24,28},{28,32},{32,36}... | collective-permute-start | bytes 20 | tf_op jit(solution)/shard_map/ppermute | solution.py:314
  11.3 1.0 copy.13.weights_ref
  13.0 1.2 copy-done.1
  14.2 1.2 copy-done.2
  15.4 1.2 copy-done.3
  18.1 15.1 %shard_map.100 = (f32[1024,512]{1,0:T(8,128)}, bf16[1024,512]{1,0:T(8,128)(2,1)S(1)}, bf16[4,144,256]{2,1,0:T(8,128)(2,1)S(1)}) custom-call(bf16[1024,512]{1,0:T(8,128)(2,1)S(1)} %copy-done.1, bf16[1024,512]{1,0:T(8,128)(2,1)S(1)} %copy-done.2, bf16[1024,512]{1,0:T(8,128)(2,1)S(1)} %copy-done.3, f32[4,1024]{1,0:T(4,128)S(1)} %copy-done.5, ...), custom_call_target="tpu_custom_call" | custom-call | flops 20000000000 | bytes 8000000 | tf_op jit(solution)/shard_map/pallas_call | solution.py:193
  35.2 2.0 %collective-permute-start.1 = (bf16[4,144,256]{2,1,0:T(8,128)(2,1)S(1)}, bf16[4,144,256]{2,1,0:T(8,128)(2,1)S(1)}, u32[]{:S(2)}, u32[]{:S(2)}) collective-permute-start(bf16[4,144,256]{2,1,0:T(8,128)(2,1)S(1)} %concatenate.66), channel_id=1, source_target_pairs={{0,4},{4,0},{8,12},{12,8},{16,20},{20,16},{24,28},{28,24},{32,36},... | collective-permute-start | bytes 884744 | tf_op jit(solution)/shard_map/ppermute | solution.py:269
  37.3 1.2 collective-permute-done.1
  39.5 2.0 %collective-permute-start.2 = (bf16[4,144,256]{2,1,0:T(8,128)(2,1)S(1)}, bf16[4,144,256]{2,1,0:T(8,128)(2,1)S(1)}, u32[]{:S(2)}, u32[]{:S(2)}) collective-permute-start(bf16[4,144,256]{2,1,0:T(8,128)(2,1)S(1)} %concatenate.69), channel_id=1, source_target_pairs={{0,8},{4,12},{8,0},{12,4},{16,24},{20,28},{24,16},{28,20},{32,40},... | collective-permute-start | bytes 884744 | tf_op jit(solution)/shard_map/ppermute | solution.py:269
  41.5 7.5 %collective-permute-done.2 = bf16[4,144,256]{2,1,0:T(8,128)(2,1)S(1)} collective-permute-done((bf16[4,144,256]{2,1,0:T(8,128)(2,1)S(1)}, bf16[4,144,256]{2,1,0:T(8,128)(2,1)S(1)}, u32[]{:S(2)}, u32[]{:S(2)}) %collective-permute-start.2) | collective-permute-done | bytes 294944 | tf_op jit(solution)/shard_map/ppermute | solution.py:269
  50.1 4.6 %collective-permute-start.3 = (bf16[4,144,256]{2,1,0:T(8,128)(2,1)S(1)}, bf16[4,144,256]{2,1,0:T(8,128)(2,1)S(1)}, u32[]{:S(2)}, u32[]{:S(2)}) collective-permute-start(bf16[4,144,256]{2,1,0:T(8,128)(2,1)S(1)} %concatenate.72), channel_id=1, source_target_pairs={{0,16},{4,20},{8,24},{12,28},{16,0},{20,4},{24,8},{28,12},{32,48},... | collective-permute-start | bytes 884744 | tf_op jit(solution)/shard_map/ppermute | solution.py:269
  54.7 13.3 %collective-permute-done.3 = bf16[4,144,256]{2,1,0:T(8,128)(2,1)S(1)} collective-permute-done((bf16[4,144,256]{2,1,0:T(8,128)(2,1)S(1)}, bf16[4,144,256]{2,1,0:T(8,128)(2,1)S(1)}, u32[]{:S(2)}, u32[]{:S(2)}) %collective-permute-start.3) | collective-permute-done | bytes 294944 | tf_op jit(solution)/shard_map/ppermute | solution.py:269
  68.3 1.0 fusion.111
  69.4 1.2 concatenate.75
  70.6 4.1 %collective-permute-start.4 = (bf16[4,144,256]{2,1,0:T(8,128)(2,1)S(1)}, bf16[4,144,256]{2,1,0:T(8,128)(2,1)S(1)}, u32[]{:S(2)}, u32[]{:S(2)}) collective-permute-start(bf16[4,144,256]{2,1,0:T(8,128)(2,1)S(1)} %concatenate.75), channel_id=1, source_target_pairs={{0,32},{4,36},{8,40},{12,44},{16,48},{20,52},{24,56},{28,60},{32,0... | collective-permute-start | bytes 884744 | tf_op jit(solution)/shard_map/ppermute | solution.py:269
  74.7 14.5 %collective-permute-done.4 = bf16[4,144,256]{2,1,0:T(8,128)(2,1)S(1)} collective-permute-done((bf16[4,144,256]{2,1,0:T(8,128)(2,1)S(1)}, bf16[4,144,256]{2,1,0:T(8,128)(2,1)S(1)}, u32[]{:S(2)}, u32[]{:S(2)}) %collective-permute-start.4) | collective-permute-done | bytes 294944 | tf_op jit(solution)/shard_map/ppermute | solution.py:269
  90.4 1.0 concatenate.78
  91.9 7.6 %collective-permute-done.5 = bf16[4,144,256]{2,1,0:T(8,128)(2,1)S(1)} collective-permute-done((bf16[4,144,256]{2,1,0:T(8,128)(2,1)S(1)}, bf16[4,144,256]{2,1,0:T(8,128)(2,1)S(1)}, u32[]{:S(2)}, u32[]{:S(2)}) %collective-permute-start.5) | collective-permute-done | bytes 294944 | tf_op jit(solution)/shard_map/ppermute | solution.py:269
  99.6 1.3 subtract_convert_fusion
  101.0 0.9 fusion.14
  102.2 3.8 %concatenate.81 = bf16[4,144,256]{2,1,0:T(8,128)(2,1)} concatenate(bf16[4,128,256]{2,1,0:T(8,128)(2,1)} %fusion.14, bf16[4,1,256]{2,1,0:T(2,128)(2,1)S(1)} %broadcast_in_dim.97, bf16[4,1,256]{2,1,0:T(2,128)(2,1)S(1)} %broadcast_in_dim.98, bf16[4,1,256]{2,1,0:T(2,128)(2,1)S(1)} %broadcast_in_dim.99, bf16[4,13,256]{2,1,0:T(8,128)(2,1)} %copy-done.8), dimensions={1} | concatenate | bytes 589824 | tf_op jit(solution)/shard_map/concatenate | solution.py:281
  106.0 2.6 %collective-permute-start.6 = (bf16[4,144,256]{2,1,0:T(8,128)(2,1)}, bf16[4,144,256]{2,1,0:T(8,128)(2,1)S(1)}, u32[]{:S(2)}, u32[]{:S(2)}) collective-permute-start(bf16[4,144,256]{2,1,0:T(8,128)(2,1)} %concatenate.81), channel_id=1, source_target_pairs={{0,128},{4,132},{8,136},{12,140},{16,144},{20,148},{24,152},{28,15... | collective-permute-start | bytes 884744 | tf_op jit(solution)/shard_map/ppermute | solution.py:269
  109.3 1.3 broadcast_select_fusion
  111.4 0.9 broadcast_select_fusion.3
  113.1 0.9 broadcast_select_fusion.2
  114.0 0.8 slice_multiply_fusion.7
  114.8 0.9 broadcast_select_fusion.1
  116.6 0.8 fusion.91.states_ref
  117.4 9.0 %shard_map.101 = bf16[1024,512]{1,0:T(8,128)(2,1)S(1)} custom-call(f32[1024,512]{1,0:T(8,128)} %get-tuple-element.80.out_ref, bf16[1024,512]{1,0:T(8,128)(2,1)S(1)} %get-tuple-element.81.read_ref, bf16[4,768,128]{2,1,0:T(8,128)(2,1)S(1)} %fusion.91.states_ref, f32[4,12,1024]{2,1,0:T(8,128)S(1)} %copy.13.weights_ref, bf16[1024,512]{1,0:T(8,128)(2,1)S(1)} %copy-done.4, ...), custom_call_target="tpu_custom_call" | custom-call | flops 2000000000 | bytes 6000000 | tf_op jit(solution)/shard_map/pallas_call | solution.py:250
  127.0 17.2 %all_to_all.19 = bf16[4,256,512]{1,2,0:T(8,128)(2,1)S(1)} all-to-all(bf16[4,256,512]{1,2,0:T(8,128)(2,1)S(1)} %copy.15), channel_id=1, replica_groups=mesh['ctx'=64,'head'=4] {'head'}, dimensions={0} | all-to-all | bytes 2097152 | tf_op jit(solution)/shard_map/all_to_all | solution.py:322
  144.1 6.7 %convolution_convert_fusion = bf16[256,2048]{1,0:T(8,128)(2,1)} fusion(bf16[256,2048]{0,1:T(8,128)(2,1)S(1)} %bitcast.12, bf16[2048,2048]{1,0:T(8,128)(2,1)} %all-gather.2.cloned.1.call-done), kind=kOutput, calls=%fused_computation | convolution fusion | flops 2148007936 | bytes 10485760 | tf_op jit(solution)/shard_map/dot_general | solution.py:323
  (106 shorter events, 11.2 us)
Async XLA Ops:
  6.5 137.6 %all-gather.2.cloned.1.call-start = ((), (), s32[]{:S(2)}) async-start(), calls=%async_computation.1 | async-start | bytes 10485760 | tf_op jit(solution)/shard_map/all_gather | solution.py:316
  8.5 24.8 %collective-permute-start = (s32[1]{0:T(128)}, s32[1]{0:T(128)}, u32[]{:S(2)}, u32[]{:S(2)}) collective-permute-start(s32[1]{0:T(128)} %add.61), channel_id=1, source_target_pairs={{0,4},{4,8},{8,12},{12,16},{16,20},{20,24},{24,28},{28,32},{32,36}... | collective-permute-start | bytes 20 | tf_op jit(solution)/shard_map/ppermute | solution.py:314
  12.3 0.7 copy-start
  13.0 1.2 copy-start.1
  14.2 1.2 copy-start.2
  15.4 1.2 copy-start.3
  16.7 0.7 copy-start.5
  17.4 0.7 copy-start.6
  34.9 34.5 %copy-start.8 = (bf16[4,13,256]{2,1,0:T(8,128)(2,1)}, bf16[4,13,256]{2,1,0:T(8,128)(2,1)S(1)}, u32[]{:S(2)}) copy-start(bf16[4,13,256]{2,1,0:T(8,128)(2,1)S(1)} %broadcast.1256) | copy-start | bytes 79876
  35.2 3.2 %collective-permute-start.1 = (bf16[4,144,256]{2,1,0:T(8,128)(2,1)S(1)}, bf16[4,144,256]{2,1,0:T(8,128)(2,1)S(1)}, u32[]{:S(2)}, u32[]{:S(2)}) collective-permute-start(bf16[4,144,256]{2,1,0:T(8,128)(2,1)S(1)} %concatenate.66), channel_id=1, source_target_pairs={{0,4},{4,0},{8,12},{12,8},{16,20},{20,16},{24,28},{28,24},{32,36},... | collective-permute-start | bytes 884744 | tf_op jit(solution)/shard_map/ppermute | solution.py:269
  38.5 10.9 %copy-start.9 = (bf16[4,144,256]{2,1,0:T(8,128)(2,1)}, bf16[4,144,256]{2,1,0:T(8,128)(2,1)S(1)}, u32[]{:S(2)}) copy-start(bf16[4,144,256]{2,1,0:T(8,128)(2,1)S(1)} %collective-permute-done.1) | copy-start | bytes 884740
  39.5 9.6 %collective-permute-start.2 = (bf16[4,144,256]{2,1,0:T(8,128)(2,1)S(1)}, bf16[4,144,256]{2,1,0:T(8,128)(2,1)S(1)}, u32[]{:S(2)}, u32[]{:S(2)}) collective-permute-start(bf16[4,144,256]{2,1,0:T(8,128)(2,1)S(1)} %concatenate.69), channel_id=1, source_target_pairs={{0,8},{4,12},{8,0},{12,4},{16,24},{20,28},{24,16},{28,20},{32,40},... | collective-permute-start | bytes 884744 | tf_op jit(solution)/shard_map/ppermute | solution.py:269
  49.2 51.8 %copy-start.10 = (f32[4]{0:T(128)}, f32[4]{0:T(128)S(1)}, u32[]{:S(2)}) copy-start(f32[4]{0:T(128)S(1)} %convert_reduce_fusion.4) | copy-start | bytes 52
  50.1 17.9 %collective-permute-start.3 = (bf16[4,144,256]{2,1,0:T(8,128)(2,1)S(1)}, bf16[4,144,256]{2,1,0:T(8,128)(2,1)S(1)}, u32[]{:S(2)}, u32[]{:S(2)}) collective-permute-start(bf16[4,144,256]{2,1,0:T(8,128)(2,1)S(1)} %concatenate.72), channel_id=1, source_target_pairs={{0,16},{4,20},{8,24},{12,28},{16,0},{20,4},{24,8},{28,12},{32,48},... | collective-permute-start | bytes 884744 | tf_op jit(solution)/shard_map/ppermute | solution.py:269
  68.1 33.9 %copy-start.11 = (f32[4]{0:T(128)}, f32[4]{0:T(128)S(1)}, u32[]{:S(2)}) copy-start(f32[4]{0:T(128)S(1)} %convert_reduce_fusion.3) | copy-start | bytes 52
  70.6 18.6 %collective-permute-start.4 = (bf16[4,144,256]{2,1,0:T(8,128)(2,1)S(1)}, bf16[4,144,256]{2,1,0:T(8,128)(2,1)S(1)}, u32[]{:S(2)}, u32[]{:S(2)}) collective-permute-start(bf16[4,144,256]{2,1,0:T(8,128)(2,1)S(1)} %concatenate.75), channel_id=1, source_target_pairs={{0,32},{4,36},{8,40},{12,44},{16,48},{20,52},{24,56},{28,60},{32,0... | collective-permute-start | bytes 884744 | tf_op jit(solution)/shard_map/ppermute | solution.py:269
  89.3 12.7 %copy-start.12 = (f32[4]{0:T(128)}, f32[4]{0:T(128)S(1)}, u32[]{:S(2)}) copy-start(f32[4]{0:T(128)S(1)} %convert_reduce_fusion.2) | copy-start | bytes 52
  89.3 0.6 copy-start.16
  91.3 8.1 %collective-permute-start.5 = (bf16[4,144,256]{2,1,0:T(8,128)(2,1)S(1)}, bf16[4,144,256]{2,1,0:T(8,128)(2,1)S(1)}, u32[]{:S(2)}, u32[]{:S(2)}) collective-permute-start(bf16[4,144,256]{2,1,0:T(8,128)(2,1)S(1)} %concatenate.78), channel_id=1, source_target_pairs={{0,64},{4,68},{8,72},{12,76},{16,80},{20,84},{24,88},{28,92},{32,9... | collective-permute-start | bytes 884744 | tf_op jit(solution)/shard_map/ppermute | solution.py:269
  99.6 2.5 %copy-start.13 = (f32[4]{0:T(128)}, f32[4]{0:T(128)S(1)}, u32[]{:S(2)}) copy-start(f32[4]{0:T(128)S(1)} %convert_reduce_fusion.1) | copy-start | bytes 52
  102.2 15.2 %copy-start.4 = (bf16[1024,512]{1,0:T(8,128)(2,1)S(1)}, bf16[1024,512]{1,0:T(8,128)(2,1)}, u32[]{:S(2)}) copy-start(bf16[1024,512]{1,0:T(8,128)(2,1)} %gate_ref.1) | copy-start | bytes 3145732
  102.2 15.2 %copy-start.7 = (f32[128]{0:T(128)S(1)}, f32[128]{0:T(128)}, u32[]{:S(2)}) copy-start(f32[128]{0:T(128)} %param.30) | copy-start | bytes 1540
  106.0 9.7 %copy-start.14 = (f32[4]{0:T(128)S(1)}, f32[4]{0:T(128)}, u32[]{:S(2)}) copy-start(f32[4]{0:T(128)} %copy-done.13) | copy-start | bytes 52
  106.0 9.8 %copy-start.15 = (f32[4]{0:T(128)S(1)}, f32[4]{0:T(128)}, u32[]{:S(2)}) copy-start(f32[4]{0:T(128)} %get-tuple-element.124) | copy-start | bytes 52
  106.0 10.1 %collective-permute-start.6 = (bf16[4,144,256]{2,1,0:T(8,128)(2,1)}, bf16[4,144,256]{2,1,0:T(8,128)(2,1)S(1)}, u32[]{:S(2)}, u32[]{:S(2)}) collective-permute-start(bf16[4,144,256]{2,1,0:T(8,128)(2,1)} %concatenate.81), channel_id=1, source_target_pairs={{0,128},{4,132},{8,136},{12,140},{16,144},{20,148},{24,152},{28,15... | collective-permute-start | bytes 884744 | tf_op jit(solution)/shard_map/ppermute | solution.py:269
Sparse Core Ops, SparseCore 0:
  37.4 87.6 all-gather.1
where the time goes:
time: 158 us
  waiting for transfers between devices  44.1 us (28%)
  Pallas kernels  24.2 us (15%)
  starting transfers between devices  18.5 us (12%)
  local copies, waits for them, and re-layouts  18 us (11%)
  blocking collectives  17.2 us (11%)
  between operations  15.7 us (10%)
  matrix products  13.7 us (9%)
  other arithmetic  6.34 us (4%)
    ppermute x6, waiting for transfers between devices, partner(): lax.ppermute(value, 'ctx', [(i, i ^ 1 << bit) for i in range(lax.axis_siz...  44.1 us
    all_to_all x1, blocking collectives, shards(): lax.all_to_all(normed, 'head', split_axis=0, concat_axis=1, tiled=True)  17.2 us
    ppermute x6, starting transfers between devices, partner(): lax.ppermute(value, 'ctx', [(i, i ^ 1 << bit) for i in range(lax.axis_siz...  15.8 us
    pallas_call x1, Pallas kernels, local_terms(): pl.pallas_call(local_kernel, grid=(HEADS_HERE,), in_specs=[tall, tall, ta...  15.1 us
    pallas_call x1, Pallas kernels, finish(): pl.pallas_call(finish_kernel, grid=(HEADS_HERE,), in_specs=[tall, tall, p...  9.02 us
    unnamed x35, local copies, waits for them, and re-layouts  7.28 us
    dot_general x11, matrix products, compose(): jnp.einsum('hij,hjk->hik', erase, body_e.astype(BF16), preferred_element_...  6.99 us
    concatenate x6, local copies, waits for them, and re-layouts, pack(): return jnp.concatenate([body.astype(BF16), *split3(wide), zeros], axis=1)  6.77 us
  transfers between devices with their start and end apart: 8, of which 5 were waited for; matrix products, arithmetic and copies ran while one was open for 15% of the time, Pallas kernels for 15%

commit v1 on v0

v1 whole, which is shorter than its diff:
```python
import jax
import jax.numpy as jnp
from jax import lax
from jax.experimental import pallas as pl
from jax.experimental.pallas import tpu as pltpu
from jax.sharding import PartitionSpec as P

BLOCK = 128
BLOCKS = 8
TOKENS_HERE = 1024
HEADS_HERE = 4
WIDTH = 128
LEVELS = 12
EPSILON = 1e-06
FAR = -1e4
MESSAGE_ROWS = 144

F32 = jnp.float32
BF16 = jnp.bfloat16


def dot(left, right):
    return jnp.dot(left, right, preferred_element_type=F32)


def dot_rows(left, right):
    return lax.dot_general(left, right, (((1,), (1,)), ((), ())), preferred_element_type=F32)


def dot_columns(left, right):
    return lax.dot_general(left, right, (((0,), (0,)), ((), ())), preferred_element_type=F32)


def split3(value):
    first = value.astype(BF16)
    rest = value - first.astype(F32)
    second = rest.astype(BF16)
    third = (rest - second.astype(F32)).astype(BF16)
    return first, second, third


def rows_of(block):
    return slice(block * BLOCK, (block + 1) * BLOCK)


def weight_column(level):
    return level if level < 8 else level + 4


def prepare_masks(seg_ref, far_ref, pair_ref):
    row = lax.broadcasted_iota(jnp.int32, (BLOCK, BLOCK), 0)
    col = lax.broadcasted_iota(jnp.int32, (BLOCK, BLOCK), 1)
    segs = seg_ref[...].astype(F32)
    padded = jnp.concatenate([segs, jnp.zeros((BLOCK - BLOCKS, BLOCK), F32)], axis=0)
    seg_cols = padded.T
    for block in range(BLOCKS):
        same = seg_cols[:, block : block + 1] == segs[block : block + 1, :]
        far_ref[block] = jnp.where(same & (row >= col), 0.0, FAR)
    for step in range(7):
        size = 1 << step
        chosen = (row // size == col // size + 1) & (row // size % 2 == 1)
        pair_ref[step] = jnp.where(chosen, 1.0, 0.0).astype(BF16)


def unit_rows(rows, ones):
    wide = rows.astype(F32)
    total = dot((wide * wide).astype(BF16), ones)
    return (wide * lax.rsqrt(total + EPSILON)).astype(BF16)


def head_terms(q, k, v, decay, strength, level_weights, segs, far_ref, pair_ref):
    row = lax.broadcasted_iota(jnp.int32, (BLOCK, BLOCK), 0)
    col = lax.broadcasted_iota(jnp.int32, (BLOCK, BLOCK), 1)
    every = range(BLOCKS)
    ones = jnp.ones((BLOCK, BLOCK), BF16)
    upto = jnp.where(row <= col, 1.0, 0.0).astype(BF16)
    summed = sum(dot(part, upto) for part in split3(decay))
    last_sum = jnp.broadcast_to(summed[:, BLOCK - 1 :], (BLOCKS, BLOCK))
    last_seg = jnp.broadcast_to(segs[:, BLOCK - 1 :], (BLOCKS, BLOCK))
    first_seg = jnp.broadcast_to(segs[:, :1], (BLOCKS, BLOCK))
    before = jnp.concatenate([first_seg[:1], last_seg[:-1]], axis=0)
    opening = jnp.exp(summed) * (segs == before).astype(F32)
    closing = jnp.exp(last_sum - summed) * (segs == last_seg).astype(F32)
    keeps = jnp.exp(last_sum) * (last_seg == before).astype(F32)
    stacked = jnp.concatenate(
        [summed, strength, opening, strength * opening, closing, jnp.zeros((BLOCK - 40, BLOCK), F32)], axis=0
    )
    cols = stacked.T
    wcols = jnp.concatenate(level_weights, axis=0).T

    def column(kind, block):
        return cols[:, kind * 8 + block : kind * 8 + block + 1]

    def weight(level, block):
        at = block * 16 + weight_column(level)
        return wcols[:, at : at + 1]

    qn = unit_rows(q, ones)
    kn = unit_rows(k, ones)
    grams = [
        dot_rows(jnp.concatenate([kn[rows_of(b)], qn[rows_of(b)]], axis=0), kn[rows_of(b)]) for b in every
    ]
    fading = [jnp.exp(column(0, b) - summed[b : b + 1, :] + far_ref[b]) for b in every]
    lower = [(column(1, b) * fading[b] * grams[b][:BLOCK]).astype(BF16) for b in every]
    scores = [(fading[b] * grams[b][BLOCK:]).astype(BF16) for b in every]
    eye = jnp.where(row == col, 1.0, 0.0).astype(BF16)
    inverse = [eye - lower[b] * pair_ref[0] for b in every]
    for step in range(1, 7):
        mask = pair_ref[step]
        half = [dot(inverse[b], lower[b] * mask).astype(BF16) for b in every]
        inverse = [inverse[b] - dot(half[b], inverse[b]).astype(BF16) for b in every]
    right = [
        jnp.concatenate(
            [
                (column(1, b) * v[rows_of(b)].astype(F32)).astype(BF16),
                (column(3, b) * kn[rows_of(b)].astype(F32)).astype(BF16),
            ],
            axis=1,
        )
        for b in every
    ]
    solved = [dot(inverse[b], right[b]).astype(BF16) for b in every]
    read = [dot(scores[b], solved[b]) for b in every]
    out = [weight(0, b) * read[b][:, :WIDTH] for b in every]
    reads = [column(2, b) * qn[rows_of(b)].astype(F32) - read[b][:, WIDTH:] for b in every]
    ended = [(column(4, b) * kn[rows_of(b)].astype(F32)).astype(BF16) for b in every]
    joined = [dot_columns(ended[b], solved[b]) for b in every]
    fresh = [joined[b][:, :WIDTH] for b in every]
    erase = [joined[b][:, WIDTH:] for b in every]
    keep = [keeps[b : b + 1] for b in every]
    for level in range(1, 4):
        span = 1 << (level - 1)
        fresh2, erase2, keep2 = [], [], []
        for pair in range(len(fresh) // 2):
            e, o = 2 * pair, 2 * pair + 1
            later = [b for b in every if b // span == o]
            stack = jnp.concatenate([reads[b] for b in later] + [erase[o]], axis=0).astype(BF16)
            both = dot(stack, jnp.concatenate([fresh[e], erase[e]], axis=1).astype(BF16))
            for at, b in enumerate(later):
                part = both[at * BLOCK : (at + 1) * BLOCK]
                out[b] = out[b] + weight(level, b) * part[:, :WIDTH]
                reads[b] = keep[e] * reads[b] - part[:, WIDTH:]
            part = both[len(later) * BLOCK :]
            fresh2.append(keep[o] * fresh[e] - part[:, :WIDTH] + fresh[o])
            erase2.append(keep[o] * erase[e] + keep[e] * erase[o] - part[:, WIDTH:])
            keep2.append(keep[e] * keep[o])
        fresh, erase, keep = fresh2, erase2, keep2
    return out, reads, fresh[0], erase[0], keep[0], wcols


def finish_block(out, read, states, columns, gate, gain, ones):
    wide = read.astype(F32)
    lhs = jnp.concatenate([(column * wide).astype(BF16) for column in columns], axis=1)
    total = out + dot(lhs, states)
    mean = dot((total * total).astype(BF16), ones) * (1.0 / WIDTH)
    gate = gate.astype(F32)
    silu = gate / (1.0 + jnp.exp(-gate))
    return (total * lax.rsqrt(mean + EPSILON) * gain * silu).astype(BF16)


STAGES = 6
HOPS = (1, 2, 4, 14, 16, 48)
STEPS = HEADS_HERE + STAGES + 1
MESH = pl.DeviceIdType.MESH


def layer_kernel(
    q_hbm,
    k_hbm,
    v_hbm,
    gate_hbm,
    w_hbm,
    decay_ref,
    strength_ref,
    weights_ref,
    seg_ref,
    gain_ref,
    result_ref,
    q_ref,
    k_ref,
    v_ref,
    gate_ref,
    whole_ref,
    far_ref,
    pair_ref,
    spread_ref,
    out_ref,
    read_ref,
    column_ref,
    normed_ref,
    gathered_ref,
    sent_ref,
    came_ref,
    total_ref,
    keep_ref,
    prefix_ref,
    prekeep_ref,
    chip_ref,
    states_ref,
    segs_ref,
    before_ref,
    load_sem,
    own_sem,
    seg_sem,
    sent_sem,
    came_sem,
    chip_sent_sem,
    chip_came_sem,
    out_sem,
    in_sem,
    w_sent_sem,
    w_came_sem,
):
    ctx = lax.axis_index("ctx")
    x = lax.axis_index("head")
    core = lax.rem(ctx, 2)
    count = lax.axis_size("ctx")
    right, left = lax.rem(x + 1, 4), lax.rem(x + 3, 4)
    after, ahead = lax.rem(ctx + 1, count), lax.rem(ctx + count - 1, count)

    def flipped(hop):
        place, rest = 0, ctx
        for bit in range(6):
            digit = lax.rem(rest, 2)
            rest = rest // 2
            place = place + ((1 - digit) if hop >> bit & 1 else digit) * (1 << bit)
        return place

    def remote(source, target, sent, came, axis, at):
        return pltpu.make_async_remote_copy(
            src_ref=source,
            dst_ref=target,
            send_sem=sent,
            recv_sem=came,
            device_id={axis: at},
            device_id_type=MESH,
        )

    partners = [("ctx", flipped(hop)) for hop in HOPS]
    partners += [("head", lax.rem(x + d, 4)) for d in (1, 2, 3)] + [("ctx", after), ("ctx", ahead)]

    sources = ((q_hbm, q_ref), (k_hbm, k_ref), (v_hbm, v_ref), (gate_hbm, gate_ref))

    def load(which, head):
        source, target = sources[which]
        columns = pl.ds(pl.multiple_of(head * WIDTH, WIDTH), WIDTH)
        return pltpu.make_async_copy(source.at[:, columns], target.at[head], load_sem.at[which, head])

    own_w = pltpu.make_async_copy(w_hbm, whole_ref.at[x], own_sem)
    quarters = [pl.ds(pl.multiple_of(core * 256 + part * 128, 128), 128) for part in range(2)]
    half = pl.ds(pl.multiple_of(core * 256, 256), 256)
    other_core = flipped(1)

    def w_copy(at, source, shard, rows, axis, to):
        return remote(source, whole_ref.at[shard, rows], w_sent_sem.at[at], w_came_sem.at[at], axis, to)

    w_first = [
        w_copy(0, w_hbm.at[quarters[0]], x, quarters[0], "head", right),
        w_copy(1, w_hbm.at[quarters[1]], x, quarters[1], "head", left),
        w_copy(2, w_hbm.at[quarters[1]], x, quarters[1], "head", right),
        w_copy(3, w_hbm.at[quarters[0]], x, quarters[0], "head", left),
    ]
    w_relay = [
        w_copy(4, whole_ref.at[left, quarters[0]], left, quarters[0], "head", right),
        w_copy(5, whole_ref.at[right, quarters[1]], right, quarters[1], "head", left),
    ]
    w_core = [
        w_copy(6 + at, whole_ref.at[shard, half], shard, half, "ctx", other_core)
        for at, shard in enumerate((left, right, lax.rem(x + 2, 4)))
    ]
    seg_copy = remote(segs_ref, before_ref, seg_sem.at[0], seg_sem.at[1], "ctx", after)

    def message(stage, head):
        return remote(
            sent_ref.at[stage, head],
            came_ref.at[stage, head],
            sent_sem.at[stage, head],
            came_sem.at[stage, head],
            "ctx",
            flipped(HOPS[stage]),
        )

    def chip_copy(head):
        return remote(
            chip_ref.at[head], chip_ref.at[head], chip_sent_sem.at[head], chip_came_sem.at[head], "ctx", other_core
        )

    def spread_copy(head, d):
        to = lax.rem(x + d, 4)
        rows = pl.ds(pl.multiple_of(to * 256, 256), 256)
        columns = pl.ds(pl.multiple_of(x * 512 + head * WIDTH, WIDTH), WIDTH)
        return remote(
            normed_ref.at[head, rows],
            gathered_ref.at[:, columns],
            out_sem.at[head, d - 1],
            in_sem.at[head, d - 1],
            "head",
            to,
        )

    def owns(head):
        return lax.rem(head, 2) == core

    def write_message(stage, head, body, keep):
        sent_ref[stage, head, :BLOCK, :] = body.astype(BF16)
        first, second, third = split3(keep)
        sent_ref[stage, head, BLOCK:, :] = jnp.concatenate(
            [first.astype(F32), second.astype(F32), third.astype(F32), jnp.zeros((13, 2 * WIDTH), F32)], axis=0
        ).astype(BF16)

    def read_keep(stage, head):
        tail = came_ref[stage, head, BLOCK:, :].astype(F32)
        return tail[0:1] + tail[1:2] + tail[2:3]

    def flag_row():
        return (before_ref[7:8, WIDTH - 1 :] == segs_ref[0:1, :1]).astype(F32)

    def store_total(head, body, keep):
        total_ref[head] = body
        keep_ref[head] = jnp.broadcast_to(keep, (8, 2 * WIDTH))

    def local_step(head):
        for which in range(3):
            load(which, head).wait()
        weights = [
            part
            for b in range(BLOCKS)
            for part in (weights_ref[head, 0:8, rows_of(b)], weights_ref[head, 4:12, rows_of(b)])
        ]
        out, reads, fresh, erase, keep, wcols = head_terms(
            q_ref[head],
            k_ref[head],
            v_ref[head],
            spread_ref[0, head],
            spread_ref[1, head],
            weights,
            segs_ref[...],
            far_ref,
            pair_ref,
        )
        column_ref[head] = wcols
        for b in range(BLOCKS):
            out_ref[head, rows_of(b), :] = out[b]
            read_ref[head, rows_of(b), :] = reads[b].astype(BF16)

        @pl.when(head == 0)
        def _():
            seg_copy.wait_recv()

        flag = jnp.broadcast_to(flag_row(), (1, WIDTH))
        body = jnp.concatenate([fresh, flag * erase], axis=1)
        keep = jnp.concatenate([flag * keep, flag * keep], axis=1)
        store_total(head, body, keep)
        write_message(0, head, body, keep)
        message(0, head).start()

    def combine(stage, head, upper, with_prefix, with_total):
        other = came_ref[stage, head, :BLOCK, :]
        other_keep = read_keep(stage, head)
        mine = total_ref[head]
        keep = keep_ref[head, 0:1, :]
        columns = slice((stage - 1) * WIDTH, stage * WIDTH)
        wide = other.astype(F32)
        if upper:
            parts = []
            if with_prefix:
                prefix = prefix_ref[head]
                parts.append(prefix.astype(BF16))
            if with_total:
                parts.append(mine[:, WIDTH:].astype(BF16))
            both = dot(jnp.concatenate(parts, axis=0) if len(parts) > 1 else parts[0], other)
            if with_prefix:
                moved = both[:BLOCK]
                prekeep = prekeep_ref[head, 0:1, :]
                chip_ref[head, :, columns] = (prekeep[:, :WIDTH] * wide[:, :WIDTH] - moved[:, :WIDTH]).astype(BF16)
                prefix_ref[head] = (
                    prekeep[:, WIDTH:] * wide[:, WIDTH:] + other_keep[:, WIDTH:] * prefix - moved[:, WIDTH:]
                )
                prekeep_ref[head] = jnp.broadcast_to(prekeep * other_keep, (8, 2 * WIDTH))
            if with_total:
                carried = jnp.concatenate([mine[:, :WIDTH], other_keep[:, WIDTH:] * mine[:, WIDTH:]], axis=1)
                body = keep * wide + carried - both[len(parts) * BLOCK - BLOCK :]
        else:
            if with_prefix:
                chip_ref[head, :, columns] = jnp.zeros((BLOCK, WIDTH), BF16)
            if with_total:
                moved = dot(other[:, WIDTH:], mine.astype(BF16))
                carried = jnp.concatenate([wide[:, :WIDTH], keep[:, WIDTH:] * wide[:, WIDTH:]], axis=1)
                body = other_keep * mine + carried - moved
        if with_total:
            keep = keep * other_keep
            store_total(head, body, keep)
            write_message(stage + 1, head, body, keep)

    def join_step(stage, head):
        last = stage == STAGES - 1

        def both_sides():
            digit = lax.rem(ctx // (1 << stage), 2)

            @pl.when(digit == 1)
            def _():
                combine(stage, head, True, stage > 0, not last)

            @pl.when(digit == 0)
            def _():
                combine(stage, head, False, stage > 0, not last)

        if stage == 0:
            message(0, head).wait_recv()

        @pl.when(owns(head))
        def _():
            if stage == 0:
                prefix_ref[head] = jnp.zeros((BLOCK, WIDTH), F32)
                prekeep_ref[head] = jnp.ones((8, 2 * WIDTH), F32)
            else:
                message(stage, head).wait_recv()
            both_sides()
            if last:
                chip_copy(head).start()
            else:
                message(stage + 1, head).start()

    def finish_step(head):
        @pl.when(jnp.logical_not(owns(head)))
        def _():
            chip_copy(head).wait_recv()

        load(3, head).wait()
        flag = jnp.broadcast_to(flag_row(), (1, WIDTH))
        chip = chip_ref[head]

        @pl.when(core == 0)
        def _():
            states_ref[:BLOCK, :] = jnp.zeros((BLOCK, WIDTH), BF16)
            for level in range(5):
                part = chip[:, level * WIDTH : (level + 1) * WIDTH].astype(F32)
                states_ref[(level + 1) * BLOCK : (level + 2) * BLOCK, :] = (flag * part).astype(BF16)

        @pl.when(core == 1)
        def _():
            other = came_ref[0, head, :BLOCK, :]
            keep = read_keep(0, head)[:, :WIDTH]
            states_ref[:BLOCK, :] = (flag * other[:, :WIDTH].astype(F32)).astype(BF16)
            moved = dot(other[:, WIDTH:], chip)
            for level in range(5):
                columns = slice(level * WIDTH, (level + 1) * WIDTH)
                part = keep * chip[:, columns].astype(F32) - moved[:, columns]
                states_ref[(level + 1) * BLOCK : (level + 2) * BLOCK, :] = (flag * part).astype(BF16)

        ones = jnp.ones((WIDTH, WIDTH), BF16)
        states = states_ref[...]
        for b in range(BLOCKS):
            columns = [
                column_ref[head, :, b * 16 + weight_column(level) : b * 16 + weight_column(level) + 1]
                for level in range(4, 10)
            ]
            normed_ref[head, rows_of(b), :] = finish_block(
                out_ref[head, rows_of(b), :],
                read_ref[head, rows_of(b), :],
                states,
                columns,
                gate_ref[head, rows_of(b), :],
                gain_ref[...],
                ones,
            )
        for d in (1, 3, 2):
            spread_copy(head, d).start()
        rows = pl.ds(pl.multiple_of(x * 256, 256), 256)
        columns = pl.ds(pl.multiple_of(x * 512 + head * WIDTH, WIDTH), WIDTH)
        gathered_ref[:, columns] = normed_ref[head, rows, :]

    for head in range(HEADS_HERE):
        for which in range(4):
            load(which, head).start()
    own_w.start()
    segs_ref[...] = seg_ref[...].astype(F32)
    barrier = pltpu.get_barrier_semaphore()
    for axis, at in partners:
        pl.semaphore_signal(barrier, inc=1, device_id={axis: at}, device_id_type=MESH)
    pl.semaphore_wait(barrier, len(partners))
    seg_copy.start()
    for copy in w_first:
        copy.start()
    prepare_masks(seg_ref, far_ref, pair_ref)
    for source, at in ((decay_ref, 0), (strength_ref, 1)):
        for each in range(HEADS_HERE):
            for b in range(BLOCKS):
                spread_ref[at, each, b : b + 1, :] = source[each : each + 1, rows_of(b)]

    def step(t, carry):
        @pl.when(t < HEADS_HERE)
        def _():
            local_step(t)

        for stage in reversed(range(STAGES)):
            head = t - 1 - stage

            @pl.when((head >= 0) & (head < HEADS_HERE))
            def _():
                join_step(stage, head)

        @pl.when(t == 5)
        def _():
            for at in range(2):
                w_first[at].wait_recv()
                w_relay[at].start()

        @pl.when(t == 7)
        def _():
            for at in range(2):
                w_first[2 + at].wait_recv()
                w_core[at].start()

        @pl.when(t >= STAGES + 1)
        def _():
            finish_step(t - STAGES - 1)

        return carry

    lax.fori_loop(0, STEPS, step, 0)
    for copy in w_relay:
        copy.wait_recv()
    w_core[2].start()
    own_w.wait()
    for copy in w_core:
        copy.wait_recv()
    for head in range(HEADS_HERE):
        for d in (1, 2, 3):
            spread_copy(head, d).wait_recv()

    def project(at, carry):
        columns = pl.ds(pl.multiple_of(at * 256, 256), 256)
        total = dot(gathered_ref[:, 0:512], whole_ref[0, :, columns])
        for shard in range(1, 4):
            total = total + dot(gathered_ref[:, shard * 512 : (shard + 1) * 512], whole_ref[shard, :, columns])
        result_ref[:, columns] = total.astype(BF16)
        return carry

    lax.fori_loop(0, 8, project, 0)
    seg_copy.wait_send()
    for copy in w_first + w_relay + w_core:
        copy.wait_send()
    for head in range(HEADS_HERE):
        message(0, head).wait_send()
        for d in (1, 2, 3):
            spread_copy(head, d).wait_send()

        @pl.when(owns(head))
        def _():
            for stage in range(1, STAGES):
                message(stage, head).wait_send()
            chip_copy(head).wait_send()


def shards(queries, keys, values, log_decay, write_strength, level_weights, segment, out_gate, norm_gain, w_out):
    far = pl.BlockSpec(memory_space=pl.ANY)
    near = pl.BlockSpec(memory_space=pltpu.VMEM)
    tall = (HEADS_HERE, TOKENS_HERE, WIDTH)
    return pl.pallas_call(
        layer_kernel,
        out_shape=jax.ShapeDtypeStruct((256, 2048), BF16),
        in_specs=[far] * 5 + [near] * 5,
        out_specs=near,
        scratch_shapes=[
            pltpu.VMEM(tall, BF16),
            pltpu.VMEM(tall, BF16),
            pltpu.VMEM(tall, BF16),
            pltpu.VMEM(tall, BF16),
            pltpu.VMEM((4, 512, 2048), BF16),
            pltpu.VMEM((BLOCKS, BLOCK, BLOCK), F32),
            pltpu.VMEM((7, BLOCK, BLOCK), BF16),
            pltpu.VMEM((2, HEADS_HERE, BLOCKS, BLOCK), F32),
            pltpu.VMEM(tall, F32),
            pltpu.VMEM(tall, BF16),
            pltpu.VMEM((HEADS_HERE, BLOCK, BLOCK), F32),
            pltpu.VMEM(tall, BF16),
            pltpu.VMEM((256, 2048), BF16),
            pltpu.VMEM((STAGES, HEADS_HERE, MESSAGE_ROWS, 2 * WIDTH), BF16),
            pltpu.VMEM((STAGES, HEADS_HERE, MESSAGE_ROWS, 2 * WIDTH), BF16),
            pltpu.VMEM((HEADS_HERE, BLOCK, 2 * WIDTH), F32),
            pltpu.VMEM((HEADS_HERE, 8, 2 * WIDTH), F32),
            pltpu.VMEM((HEADS_HERE, BLOCK, WIDTH), F32),
            pltpu.VMEM((HEADS_HERE, 8, 2 * WIDTH), F32),
            pltpu.VMEM((HEADS_HERE, BLOCK, 5 * WIDTH), BF16),
            pltpu.VMEM((6 * BLOCK, WIDTH), BF16),
            pltpu.VMEM((BLOCKS, BLOCK), F32),
            pltpu.VMEM((BLOCKS, BLOCK), F32),
            pltpu.SemaphoreType.DMA((4, HEADS_HERE)),
            pltpu.SemaphoreType.DMA,
            pltpu.SemaphoreType.DMA((2,)),
            pltpu.SemaphoreType.DMA((STAGES, HEADS_HERE)),
            pltpu.SemaphoreType.DMA((STAGES, HEADS_HERE)),
            pltpu.SemaphoreType.DMA((HEADS_HERE,)),
            pltpu.SemaphoreType.DMA((HEADS_HERE,)),
            pltpu.SemaphoreType.DMA((HEADS_HERE, 3)),
            pltpu.SemaphoreType.DMA((HEADS_HERE, 3)),
            pltpu.SemaphoreType.DMA((9,)),
            pltpu.SemaphoreType.DMA((9,)),
        ],
        compiler_params=pltpu.CompilerParams(
            collective_id=0, has_side_effects=True, vmem_limit_bytes=52 << 20
        ),
        cost_estimate=pl.CostEstimate(flops=24_000_000_000, bytes_accessed=16_000_000, transcendentals=0),
    )(
        queries,
        keys,
        values,
        out_gate,
        w_out,
        log_decay,
        write_strength,
        level_weights,
        segment.reshape(BLOCKS, BLOCK),
        norm_gain.reshape(1, WIDTH),
    )


def solution(mesh):
    placed = (
        P("ctx", "head"),
        P("ctx", "head"),
        P("ctx", "head"),
        P("head", "ctx"),
        P("head", "ctx"),
        P("head", None, "ctx"),
        P("ctx"),
        P("ctx", "head"),
        P(),
        P("head", None),
    )
    return jax.shard_map(
        shards, mesh=mesh, in_specs=placed, out_specs=P(("ctx", "head"), None), check_vma=False
    )
```

time: 158 us -> 70.2 us (0.44)
  waiting for transfers between devices: 44.1 us -> 0 us
  Pallas kernels: 24.2 us -> 64.5 us
  starting transfers between devices: 18.5 us -> 0 us
  blocking collectives: 17.2 us -> 0 us
  between operations: 15.7 us -> 0.02 us
  matrix products: 13.7 us -> 0 us
  local copies, waits for them, and re-layouts: 18 us -> 4.79 us
  other arithmetic: 6.34 us -> 0 us
    ppermute x7 -> x0, waiting for transfers between devices: 44.1 us -> none  [the longest x6 44.1 us: partner(): lax.ppermute(value, 'ctx', [(i, i ^ 1 << bit) for i in range(lax.axis_siz...]
    pallas_call x2 -> x1, Pallas kernels: 24.2 us -> 64.5 us  [shards(): pl.pallas_call(layer_kernel, out_shape=jax.ShapeDtypeStruct((256, 2048),...]
    ppermute x7 -> x0, starting transfers between devices: 18.5 us -> none  [the longest x6 15.8 us: partner(): lax.ppermute(value, 'ctx', [(i, i ^ 1 << bit) for i in range(lax.axis_siz...]
    all_to_all x1 -> x0, blocking collectives: 17.2 us -> none  [shards(): lax.all_to_all(normed, 'head', split_axis=0, concat_axis=1, tiled=True)]
    dot_general x12 -> x0, matrix products: 13.7 us -> none  [the longest x11 6.99 us: compose(): jnp.einsum('hij,hjk->hik', erase, body_e.astype(BF16), preferred_element_...]
    concatenate x6 -> x0, local copies, waits for them, and re-layouts: 6.77 us -> none  [pack(): return jnp.concatenate([body.astype(BF16), *split3(wide), zeros], axis=1)]
    unnamed x35 -> x10, local copies, waits for them, and re-layouts: 7.28 us -> 4.79 us
    mul x5 -> x0, other arithmetic: 2.4 us -> none  [compose(): keep_e * body_l[:, :, WIDTH:]]
  transfers between devices with their start and end apart: 8 -> 0, of which waited for: 5 -> 0; matrix products, arithmetic and copies ran while one was open for 15% -> 0% of each run, Pallas kernels for 15% -> 0%
where the time goes in v1:
time: 70.2 us; the launch traced here: 69.3 us
  Pallas kernels  64.5 us (92%)
  local copies, waits for them, and re-layouts  4.79 us (7%)
    pallas_call x1, Pallas kernels, shards(): pl.pallas_call(layer_kernel, out_shape=jax.ShapeDtypeStruct((256, 2048),...  64.5 us
    unnamed x10, local copies, waits for them, and re-layouts  4.79 us

profile of v1, /device:TPU:8, one launch (start us, length us, event | category | flops | bytes accessed | tf_op | source)
XLA Modules:
  0.0 69.3 jit_solution(9639438599741709801)
XLA Ops:
  0.0 1.0 %copy.11.weights_ref = f32[4,12,1024]{2,1,0:T(8,128)S(1)} copy(f32[4,12,1024]{2,0,1:T(4,128)} %param.15) | data formatting | bytes 393216 | tf_op args[5]
  1.0 0.0 copy-start
  1.1 0.7 %copy-done = f32[4,1024]{1,0:T(4,128)S(1)} copy-done((f32[4,1024]{1,0:T(4,128)S(1)}, f32[4,1024]{1,0:T(4,128)}, u32[]{:S(2)}) %copy-start) | copy-done | bytes 16408
  1.8 0.0 copy-start.1
  1.8 0.7 %copy-done.1 = f32[4,1024]{1,0:T(4,128)S(1)} copy-done((f32[4,1024]{1,0:T(4,128)S(1)}, f32[4,1024]{1,0:T(4,128)}, u32[]{:S(2)}) %copy-start.1) | copy-done | bytes 16408
  2.5 0.0 copy-start.2
  2.5 0.7 copy-done.2
  3.2 0.0 copy-start.3
  3.2 0.7 copy-done.3
  3.8 64.5 %shard_map.100 = bf16[256,2048]{1,0:T(8,128)(2,1)S(1)} custom-call(bf16[1024,512]{1,0:T(8,128)(2,1)} %q_hbm.1, bf16[1024,512]{1,0:T(8,128)(2,1)} %k_hbm.1, bf16[1024,512]{1,0:T(8,128)(2,1)} %v_hbm.1, bf16[1024,512]{1,0:T(8,128)(2,1)} %gate_hbm.1, bf16[512,2048]{1,0:T(8,128)(2,1)} %w_hbm.1, f32[4,1024]{1,0:T(4,128)S(1)} %copy-done, f32[4,1024]{1,0:T(4,128)S(1)} %copy-done.1, ...), custom_call_target="tpu_custom_call" | custom-call | flops 24000000000 | bytes 16000000 | tf_op jit(solution)/shard_map/pallas_call | solution.py:561
  68.3 1.0 %copy.13 = bf16[256,2048]{1,0:T(8,128)(2,1)} copy(bf16[256,2048]{1,0:T(8,128)(2,1)S(1)} %shard_map.100) | data formatting | bytes 2097152
Async XLA Ops:
  1.0 0.7 %copy-start = (f32[4,1024]{1,0:T(4,128)S(1)}, f32[4,1024]{1,0:T(4,128)}, u32[]{:S(2)}) copy-start(f32[4,1024]{1,0:T(4,128)} %decay_ref.1) | copy-start | bytes 49156
  1.8 0.7 %copy-start.1 = (f32[4,1024]{1,0:T(4,128)S(1)}, f32[4,1024]{1,0:T(4,128)}, u32[]{:S(2)}) copy-start(f32[4,1024]{1,0:T(4,128)} %strength_ref.1) | copy-start | bytes 49156
  2.5 0.7 copy-start.2
  3.2 0.7 copy-start.3

commit v2 on v1

v2 whole, which is shorter than its diff:
```python
import jax
import jax.numpy as jnp
from jax import lax
from jax.experimental import pallas as pl
from jax.experimental.pallas import tpu as pltpu
from jax.sharding import PartitionSpec as P

BLOCK = 128
BLOCKS = 8
TOKENS_HERE = 1024
HEADS_HERE = 4
WIDTH = 128
LEVELS = 12
EPSILON = 1e-06
FAR = -1e4
MESSAGE_ROWS = 144

F32 = jnp.float32
BF16 = jnp.bfloat16


def dot(left, right):
    return jnp.dot(left, right, preferred_element_type=F32)


def dot_rows(left, right):
    return lax.dot_general(left, right, (((1,), (1,)), ((), ())), preferred_element_type=F32)


def dot_columns(left, right):
    return lax.dot_general(left, right, (((0,), (0,)), ((), ())), preferred_element_type=F32)


def split3(value):
    first = value.astype(BF16)
    rest = value - first.astype(F32)
    second = rest.astype(BF16)
    third = (rest - second.astype(F32)).astype(BF16)
    return first, second, third


def rows_of(block):
    return slice(block * BLOCK, (block + 1) * BLOCK)


def prepare_masks(seg_ref, far_ref, pair_ref):
    row = lax.broadcasted_iota(jnp.int32, (BLOCK, BLOCK), 0)
    col = lax.broadcasted_iota(jnp.int32, (BLOCK, BLOCK), 1)
    segs = seg_ref[...].astype(F32)
    padded = jnp.concatenate([segs, jnp.zeros((BLOCK - BLOCKS, BLOCK), F32)], axis=0)
    seg_cols = padded.T
    for block in range(BLOCKS):
        same = seg_cols[:, block : block + 1] == segs[block : block + 1, :]
        far_ref[block] = jnp.where(same & (row >= col), 0.0, FAR)
    for step in range(7):
        size = 1 << step
        chosen = (row // size == col // size + 1) & (row // size % 2 == 1)
        pair_ref[step] = jnp.where(chosen, 1.0, 0.0).astype(BF16)


def unit_rows(rows, ones):
    wide = rows.astype(F32)
    total = dot((wide * wide).astype(BF16), ones)
    return (wide * lax.rsqrt(total + EPSILON)).astype(BF16)


def columns_of(rows):
    return jnp.concatenate([rows, jnp.zeros((BLOCK - rows.shape[0], BLOCK), F32)], axis=0).T


def column_at(columns, kind, block):
    at = kind * BLOCKS + block
    return columns[:, at : at + 1]


def summary_terms(heads, k_ref, v_ref, spread_ref, segs, far_ref, pair_ref, keys_ref, fading_ref, solved_ref, node_ref, keeps_ref, column_ref, between):
    row = lax.broadcasted_iota(jnp.int32, (BLOCK, BLOCK), 0)
    col = lax.broadcasted_iota(jnp.int32, (BLOCK, BLOCK), 1)
    every = range(BLOCKS)
    all_blocks = [(h, b) for h in range(len(heads)) for b in every]
    ones = jnp.ones((BLOCK, BLOCK), BF16)
    upto = jnp.where(row <= col, 1.0, 0.0).astype(BF16)
    last_seg = jnp.broadcast_to(segs[:, BLOCK - 1 :], (BLOCKS, BLOCK))
    first_seg = jnp.broadcast_to(segs[:, :1], (BLOCKS, BLOCK))
    before = jnp.concatenate([first_seg[:1], last_seg[:-1]], axis=0)
    opens = (segs == before).astype(F32)
    closes = (segs == last_seg).astype(F32)
    through = (last_seg == before).astype(F32)
    summed, columns, keep = [], [], []
    for head in heads:
        strength = spread_ref[1, head]
        total = sum(dot(part, upto) for part in split3(spread_ref[0, head]))
        last_sum = jnp.broadcast_to(total[:, BLOCK - 1 :], (BLOCKS, BLOCK))
        opening = jnp.exp(total) * opens
        closing = jnp.exp(last_sum - total) * closes
        keeps = jnp.exp(last_sum) * through
        columns.append(
            columns_of(jnp.concatenate([total, strength, opening, strength * opening, closing], axis=0))
        )
        summed.append(total)
        keep.append([keeps[b : b + 1] for b in every])
        column_ref[head] = columns[-1]
    kn = {}
    for h, head in enumerate(heads):
        unit = unit_rows(k_ref[head], ones)
        for b in every:
            kn[h, b] = unit[rows_of(b)]
    grams = {i: dot_rows(kn[i], kn[i]) for i in all_blocks}
    lower = {}
    for h, b in all_blocks:
        fading = jnp.exp(column_at(columns[h], 0, b) - summed[h][b : b + 1, :] + far_ref[b])
        fading_ref[heads[h], b] = fading
        lower[h, b] = (column_at(columns[h], 1, b) * fading * grams[h, b]).astype(BF16)
    between()
    eye = jnp.where(row == col, 1.0, 0.0).astype(BF16)
    inverse = {i: eye - lower[i] * pair_ref[0] for i in all_blocks}
    for step in range(1, 7):
        mask = pair_ref[step]
        half = {i: dot(inverse[i], lower[i] * mask).astype(BF16) for i in all_blocks}
        inverse = {i: inverse[i] - dot(half[i], inverse[i]).astype(BF16) for i in all_blocks}
    joined = {}
    for h, b in all_blocks:
        wide = kn[h, b].astype(F32)
        right = jnp.concatenate(
            [
                (column_at(columns[h], 1, b) * v_ref[heads[h], rows_of(b), :].astype(F32)).astype(BF16),
                (column_at(columns[h], 3, b) * wide).astype(BF16),
            ],
            axis=1,
        )
        solved = dot(inverse[h, b], right).astype(BF16)
        solved_ref[heads[h], b] = solved
        ended = (column_at(columns[h], 4, b) * wide).astype(BF16)
        joined[h, b] = dot_columns(ended, solved)
        keys_ref[heads[h], rows_of(b), :] = kn[h, b]
    nodes = [[joined[h, b] for b in every] for h in range(len(heads))]
    first = 0
    for level in range(3):
        many = len(nodes[0]) // 2
        for h, head in enumerate(heads):
            merged, kept = [], []
            for pair in range(many):
                early, late = nodes[h][2 * pair], nodes[h][2 * pair + 1]
                keep_e, keep_o = keep[h][2 * pair], keep[h][2 * pair + 1]
                node = early.astype(BF16)
                node_ref[head, first + pair] = node
                keeps_ref[head, first + pair : first + pair + 1, :] = keep_e
                moved = dot(late[:, WIDTH:].astype(BF16), node)
                carried = jnp.concatenate([late[:, :WIDTH], keep_e * late[:, WIDTH:]], axis=1)
                merged.append(jnp.concatenate([keep_o, keep_o], axis=1) * early + carried - moved)
                kept.append(keep_e * keep_o)
            nodes[h], keep[h] = merged, kept
        first = first + many
    return [(nodes[h][0], keep[h][0]) for h in range(len(heads))]


def readout_terms(head, q_ref, weight_ref, keys_ref, fading_ref, solved_ref, node_ref, keeps_ref, column_ref, out_ref, weighted_ref):
    every = range(BLOCKS)
    ones = jnp.ones((BLOCK, BLOCK), BF16)
    columns = column_ref[head]
    wcols = weight_ref[head].T

    def weight(level, block):
        at = block * 16 + level
        return wcols[:, at : at + 1]

    qn = unit_rows(q_ref[head], ones)
    scores = [
        (fading_ref[head, b] * dot_rows(qn[rows_of(b)], keys_ref[head, rows_of(b), :])).astype(BF16) for b in every
    ]
    both = [dot(scores[b], solved_ref[head, b]) for b in every]
    out = [weight(0, b) * both[b][:, :WIDTH] for b in every]
    reads = [column_at(columns, 2, b) * qn[rows_of(b)].astype(F32) - both[b][:, WIDTH:] for b in every]
    first = 0
    for level in range(1, 4):
        span = 1 << (level - 1)
        many = BLOCKS // (2 * span)
        for pair in range(many):
            later = [b for b in every if b // span == 2 * pair + 1]
            stack = jnp.concatenate([reads[b] for b in later], axis=0).astype(BF16)
            moved = dot(stack, node_ref[head, first + pair])
            keep = keeps_ref[head, first + pair : first + pair + 1, :]
            for at, b in enumerate(later):
                part = moved[at * BLOCK : (at + 1) * BLOCK]
                out[b] = out[b] + weight(level, b) * part[:, :WIDTH]
                reads[b] = keep * reads[b] - part[:, WIDTH:]
        first = first + many
    for b in every:
        out_ref[head, rows_of(b), :] = out[b]
        weighted_ref[head, rows_of(b), :] = jnp.concatenate(
            [(weight(level, b) * reads[b]).astype(BF16) for level in range(4, 10)], axis=1
        )

MESH = pl.DeviceIdType.MESH
GROUPS = 2


def joined(late, early):
    keep_l, body_l = late
    keep_e, body_e = early
    moved = dot(body_l[:, WIDTH:].astype(BF16), body_e.astype(BF16))
    carried = jnp.concatenate([body_l[:, :WIDTH], keep_e[:, WIDTH:] * body_l[:, WIDTH:]], axis=1)
    return keep_l * keep_e, keep_l * body_e + carried - moved


def without_state(summary):
    keep, body = summary
    return keep, jnp.concatenate([jnp.zeros((BLOCK, WIDTH), F32), body[:, WIDTH:]], axis=1)


def keep_rows(keep):
    first, second, third = split3(keep)
    return jnp.concatenate(
        [first.astype(F32), second.astype(F32), third.astype(F32), jnp.zeros((13, 2 * WIDTH), F32)], axis=0
    ).astype(BF16)


def layer_kernel(
    q_hbm,
    k_hbm,
    v_hbm,
    gate_hbm,
    w_hbm,
    decay_hbm,
    strength_hbm,
    weights_hbm,
    seg_hbm,
    gain_hbm,
    result_ref,
    q_ref,
    k_ref,
    v_ref,
    gate_ref,
    whole_ref,
    decay_ref,
    strength_ref,
    weights_ref,
    seg_ref,
    gain_ref,
    far_ref,
    pair_ref,
    spread_ref,
    weight_ref,
    keys_ref,
    fading_ref,
    solved_ref,
    node_ref,
    keeps_ref,
    column_ref,
    out_ref,
    weighted_ref,
    silu_ref,
    normed_ref,
    gathered_ref,
    sum_ref,
    core_sent_ref,
    core_came_ref,
    quad_ref,
    oct_sent_ref,
    oct_ref,
    total_ref,
    keep_ref,
    prefix_ref,
    prekeep_ref,
    chip_ref,
    segs_ref,
    before_ref,
    load_sem,
    small_sem,
    own_sem,
    seg_sem,
    core_sem,
    quad_sem,
    oct_sem,
    chip_sem,
    out_sem,
    in_sem,
    w_sent_sem,
    w_came_sem,
):
    ctx = lax.axis_index("ctx")
    x = lax.axis_index("head")
    core = lax.rem(ctx, 2)
    z = lax.rem(ctx // 2, 8)
    y = ctx // 16
    zq = lax.rem(z, 4)
    zh = z // 4
    place = 2 * y + zh
    count = lax.axis_size("ctx")
    right, left = lax.rem(x + 1, 4), lax.rem(x + 3, 4)
    after, ahead = lax.rem(ctx + 1, count), lax.rem(ctx + count - 1, count)
    other_core = ctx + 1 - 2 * core

    def at(y_to, z_to):
        return (y_to * 8 + z_to) * 2 + core

    def quad_to(d):
        return at(y, zh * 4 + lax.rem(zq + d, 4))

    def oct_to(d):
        to = lax.rem(place + d, 8)
        half = lax.rem(to, 2)
        across = zh + half - 2 * zh * half
        return at(to // 2, z + across * (7 - 2 * z))

    def remote(source, target, sent, came, axis, to):
        return pltpu.make_async_remote_copy(
            src_ref=source,
            dst_ref=target,
            send_sem=sent,
            recv_sem=came,
            device_id={axis: to},
            device_id_type=MESH,
        )

    partners = [("ctx", other_core), ("ctx", after), ("ctx", ahead)]
    partners += [("ctx", quad_to(d)) for d in (1, 2, 3)]
    partners += [("ctx", oct_to(d)) for d in range(1, 8)]
    partners += [("head", lax.rem(x + d, 4)) for d in (1, 2, 3)]

    sources = ((k_hbm, k_ref), (v_hbm, v_ref), (q_hbm, q_ref), (gate_hbm, gate_ref))

    def load(which, head):
        source, target = sources[which]
        columns = slice(head * WIDTH, (head + 1) * WIDTH)
        return pltpu.make_async_copy(source.at[:, columns], target.at[head], load_sem.at[which, head])

    smalls = [
        pltpu.make_async_copy(source, target, small_sem.at[n])
        for n, (source, target) in enumerate(
            (
                (seg_hbm, seg_ref),
                (decay_hbm, decay_ref),
                (strength_hbm, strength_ref),
                (weights_hbm, weights_ref),
                (gain_hbm, gain_ref),
            )
        )
    ]
    own_w = pltpu.make_async_copy(w_hbm, whole_ref.at[x], own_sem)
    quarters = [pl.ds(pl.multiple_of(core * 256 + part * 128, 128), 128) for part in range(2)]
    half_rows = pl.ds(pl.multiple_of(core * 256, 256), 256)

    def w_copy(n, source, shard, rows, axis, to):
        return remote(source, whole_ref.at[shard, rows], w_sent_sem.at[n], w_came_sem.at[n], axis, to)

    w_first = [
        w_copy(0, w_hbm.at[quarters[0]], x, quarters[0], "head", right),
        w_copy(1, w_hbm.at[quarters[1]], x, quarters[1], "head", left),
        w_copy(2, w_hbm.at[quarters[1]], x, quarters[1], "head", right),
        w_copy(3, w_hbm.at[quarters[0]], x, quarters[0], "head", left),
    ]
    w_relay = [
        w_copy(4, whole_ref.at[left, quarters[0]], left, quarters[0], "head", right),
        w_copy(5, whole_ref.at[right, quarters[1]], right, quarters[1], "head", left),
    ]
    w_core = [
        w_copy(6 + n, whole_ref.at[shard, half_rows], shard, half_rows, "ctx", other_core)
        for n, shard in enumerate((left, right, lax.rem(x + 2, 4)))
    ]
    seg_copy = remote(segs_ref, before_ref, seg_sem.at[0], seg_sem.at[1], "ctx", after)

    def core_copy(head):
        return remote(
            core_sent_ref.at[head], core_came_ref.at[head], core_sem.at[0, head], core_sem.at[1, head], "ctx", other_core
        )

    def quad_copy(group, d):
        mine = quad_ref.at[group, zq]
        return remote(mine, mine, quad_sem.at[0, group, d - 1], quad_sem.at[1, group, d - 1], "ctx", quad_to(d))

    def oct_copy(group, d):
        return remote(
            oct_sent_ref.at[group],
            oct_ref.at[group, place],
            oct_sem.at[0, group, d - 1],
            oct_sem.at[1, group, d - 1],
            "ctx",
            oct_to(d),
        )

    def chip_copy(group, part, head):
        mine = chip_ref.at[head, pl.ds(2 * part, 2 + part)]
        return remote(mine, mine, chip_sem.at[0, group, part], chip_sem.at[1, group, part], "ctx", other_core)

    def spread_copy(head, d):
        to = lax.rem(x + d, 4)
        rows = pl.ds(pl.multiple_of(to * 256, 256), 256)
        columns = pl.ds(pl.multiple_of(x * 512 + head * WIDTH, WIDTH), WIDTH)
        return remote(
            normed_ref.at[head, rows],
            gathered_ref.at[:, columns],
            out_sem.at[head, d - 1],
            in_sem.at[head, d - 1],
            "head",
            to,
        )

    def own_head(group):
        return 2 * group + core

    def read(ref):
        tail = ref[BLOCK:, :].astype(F32)
        return tail[0:1] + tail[1:2] + tail[2:3], ref[:BLOCK, :].astype(F32)

    def write(ref, summary):
        keep, body = summary
        ref[:BLOCK, :] = body.astype(BF16)
        ref[BLOCK:, :] = keep_rows(keep)

    def flag_row():
        same = (before_ref[7:8, WIDTH - 1 :] == segs_ref[0:1, :1]).astype(F32)
        return jnp.broadcast_to(same, (1, WIDTH))

    def summary_step(group, between):
        heads = [2 * group, 2 * group + 1]
        for head in heads:
            for which in range(2):
                load(which, head).wait()
        found = summary_terms(
            heads,
            k_ref,
            v_ref,
            spread_ref,
            segs_ref[...],
            far_ref,
            pair_ref,
            keys_ref,
            fading_ref,
            solved_ref,
            node_ref,
            keeps_ref,
            column_ref,
            between,
        )
        if group == 0:
            seg_copy.wait_recv()
        flag = flag_row()
        for head, (body, keep) in zip(heads, found):
            keep = jnp.concatenate([flag * keep, flag * keep], axis=1)
            body = jnp.concatenate([body[:, :WIDTH], flag * body[:, WIDTH:]], axis=1)
            total_ref[head] = body
            keep_ref[head] = jnp.broadcast_to(keep, (8, 2 * WIDTH))
            write(core_sent_ref.at[head], (keep, body))
            core_copy(head).start()

    def chip_step(group):
        for head in (2 * group, 2 * group + 1):
            core_copy(head).wait_recv()
        head = own_head(group)
        mine = keep_ref[head, 0:1, :], total_ref[head]
        other = read(core_came_ref.at[head])
        to = quad_ref.at[group, zq]

        @pl.when(core == 1)
        def _():
            write(to, joined(mine, other))

        @pl.when(core == 0)
        def _():
            write(to, joined(other, mine))

        for d in (1, 3, 2):
            quad_copy(group, d).start()

    def quad_step(group):
        for d in (1, 2, 3):
            quad_copy(group, d).wait_recv()
        parts = [read(quad_ref.at[group, n]) for n in range(4)]
        first, second = joined(parts[1], parts[0]), joined(parts[3], parts[2])
        write(oct_sent_ref.at[group], joined(second, first))
        for d in range(1, 8):

            @pl.when(place + d < 8)
            def _():
                oct_copy(group, d).start()

        head = own_head(group)
        odd = lax.rem(zq, 2)
        upper = zq // 2
        keep, body = read(quad_ref.at[group, odd * (zq - odd)])
        odd, upper = odd.astype(F32), upper.astype(F32)
        keep, body = odd * keep + (1.0 - odd), odd * body
        chip_ref[head, 0] = body[:, :WIDTH].astype(BF16)
        before = without_state((keep, body))
        over_keep, over = joined(before, first)
        chip_ref[head, 1] = (upper * over[:, :WIDTH]).astype(BF16)
        chip_copy(group, 0, head).start()
        keep = upper * over_keep + (1.0 - upper) * before[0]
        prekeep_ref[group] = jnp.broadcast_to(keep, (8, 2 * WIDTH))
        prefix_ref[group] = upper * over + (1.0 - upper) * before[1]

    def oct_step(group):
        for d in range(1, 8):

            @pl.when(place >= d)
            def _():
                oct_copy(group, d).wait_recv()

        head = own_head(group)
        odd, upper = lax.rem(y, 2), y // 2

        def slot(use, n):
            return read(oct_ref.at[group, use * n + (1 - use) * 7])

        prefix = without_state((prekeep_ref[group, 0:1, :], prefix_ref[group]))
        sibling = joined(slot(odd, 2 * y - 1), slot(odd, 2 * y - 2))
        pair = joined(slot(upper, 1), slot(upper, 0)), joined(slot(upper, 3), slot(upper, 2))
        over = joined(prefix, slot(zh, place - 1))
        oldest = joined(pair[1], pair[0])
        chip_ref[head, 2] = over[1][:, :WIDTH].astype(BF16)
        over = joined(without_state(over), sibling)
        chip_ref[head, 3] = over[1][:, :WIDTH].astype(BF16)
        over = joined(without_state(over), oldest)
        chip_ref[head, 4] = over[1][:, :WIDTH].astype(BF16)
        chip_copy(group, 1, head).start()

    def readout_step(head):
        load(2, head).wait()
        readout_terms(
            head,
            q_ref,
            weight_ref,
            keys_ref,
            fading_ref,
            solved_ref,
            node_ref,
            keeps_ref,
            column_ref,
            out_ref,
            weighted_ref,
        )

    def gate_step(head):
        load(3, head).wait()
        gate = gate_ref[head].astype(F32)
        silu_ref[head] = gate / (1.0 + jnp.exp(-gate)) * gain_ref[...]

    def own_states(head, first, last):
        later = core.astype(F32)
        keep, body = read(core_came_ref.at[head])
        keep = later * keep[:, :WIDTH] + (1.0 - later)
        erase = (later * body[:, WIDTH:]).astype(BF16)
        states = [chip_ref[head, n] for n in range(first, last)]
        moved = dot(erase, jnp.concatenate(states, axis=1))
        flag = flag_row()
        carried = [
            (flag * (keep * state.astype(F32) - moved[:, n * WIDTH : (n + 1) * WIDTH])).astype(BF16)
            for n, state in enumerate(states)
        ]
        if first == 0:
            carried = [(flag * later * body[:, :WIDTH]).astype(BF16)] + carried
        return jnp.concatenate(carried, axis=0)

    def await_states(group, part, head):
        @pl.when(head != own_head(group))
        def _():
            chip_copy(group, part, head).wait_recv()

    def near_step(group, head):
        await_states(group, 0, head)
        states = own_states(head, 0, 2)
        out_ref[head] += dot(weighted_ref[head, :, : 3 * WIDTH], states)

    def finish_step(group, head):
        await_states(group, 1, head)
        states = own_states(head, 2, 5)
        ones = jnp.ones((WIDTH, WIDTH), BF16)
        total = out_ref[head] + dot(weighted_ref[head, :, 3 * WIDTH :], states)
        mean = dot((total * total).astype(BF16), ones) * (1.0 / WIDTH)
        normed_ref[head] = (total * lax.rsqrt(mean + EPSILON) * silu_ref[head]).astype(BF16)
        for d in (2, 1, 3):
            spread_copy(head, d).start()
        rows = pl.ds(pl.multiple_of(x * 256, 256), 256)
        columns = pl.ds(pl.multiple_of(x * 512 + head * WIDTH, WIDTH), WIDTH)
        gathered_ref[:, columns] = normed_ref[head, rows, :]

    def finish_group(group):
        for turn in range(2):
            @pl.when(core == 0)
            def _():
                finish_step(group, 2 * group + turn)

            @pl.when(core == 1)
            def _():
                finish_step(group, 2 * group + 1 - turn)

    def project_group(group):
        for head in (2 * group, 2 * group + 1):
            for d in (1, 2, 3):
                spread_copy(head, d).wait_recv()

        def tile(n, carry):
            columns = pl.ds(pl.multiple_of(n * 256, 256), 256)
            rows = slice(group * 256, (group + 1) * 256)
            total = sum(
                dot(gathered_ref[:, shard * 512 + group * 256 : shard * 512 + (group + 1) * 256], whole_ref[shard, rows, columns])
                for shard in range(4)
            )
            if group == 0:
                sum_ref[:, columns] = total
            else:
                result_ref[:, columns] = (total + sum_ref[:, columns]).astype(BF16)
            return carry

        lax.fori_loop(0, 8, tile, 0)

    for copy in smalls[:3]:
        copy.start()
    for head in range(HEADS_HERE):
        for which in range(2):
            load(which, head).start()
    for copy in smalls[3:]:
        copy.start()
    for head in range(HEADS_HERE):
        for which in (2, 3):
            load(which, head).start()
    own_w.start()
    for group in range(GROUPS):
        for n in range(8):
            oct_ref[group, n, :BLOCK, :] = jnp.zeros((BLOCK, 2 * WIDTH), BF16)
            oct_ref[group, n, BLOCK:, :] = keep_rows(jnp.ones((1, 2 * WIDTH), F32))
    barrier = pltpu.get_barrier_semaphore()
    for axis, to in partners:
        pl.semaphore_signal(barrier, inc=1, device_id={axis: to}, device_id_type=MESH)
    smalls[0].wait()
    segs_ref[...] = seg_ref[...].astype(F32)
    prepare_masks(seg_ref, far_ref, pair_ref)
    for source, n in ((decay_ref, 0), (strength_ref, 1)):
        smalls[1 + n].wait()
        for each in range(HEADS_HERE):
            for b in range(BLOCKS):
                spread_ref[n, each, b : b + 1, :] = source[each : each + 1, rows_of(b)]
    pl.semaphore_wait(barrier, len(partners))
    seg_copy.start()
    for copy in w_first:
        copy.start()

    summary_step(0, lambda: None)
    summary_step(1, lambda: chip_step(0))
    for copy in smalls[3:]:
        copy.wait()
    for level in range(10):
        for each in range(HEADS_HERE):
            for b in range(BLOCKS):
                row = b * 16 + level
                weight_ref[each, row : row + 1, :] = weights_ref[level, each : each + 1, rows_of(b)]
    gate_step(0)
    chip_step(1)
    for n in range(2):
        w_first[n].wait_recv()
        w_relay[n].start()
    readout_step(0)
    quad_step(0)
    for head in range(1, HEADS_HERE):
        readout_step(head)
    quad_step(1)
    for n in range(2):
        w_first[2 + n].wait_recv()
        w_core[n].start()
    for head in range(1, HEADS_HERE):
        gate_step(head)
    near_step(0, 0)
    near_step(0, 1)
    oct_step(0)
    near_step(1, 2)
    near_step(1, 3)
    finish_group(0)
    for copy in w_relay:
        copy.wait_recv()
    w_core[2].start()
    oct_step(1)
    finish_group(1)
    own_w.wait()
    for copy in w_core:
        copy.wait_recv()
    project_group(0)
    project_group(1)
    seg_copy.wait_send()
    for copy in w_first + w_relay + w_core:
        copy.wait_send()
    for head in range(HEADS_HERE):
        core_copy(head).wait_send()
        for d in (1, 2, 3):
            spread_copy(head, d).wait_send()
    for group in range(GROUPS):
        for d in (1, 2, 3):
            quad_copy(group, d).wait_send()
        for part in range(2):
            chip_copy(group, part, own_head(group)).wait_send()
        for d in range(1, 8):

            @pl.when(place + d < 8)
            def _():
                oct_copy(group, d).wait_send()


def shards(queries, keys, values, log_decay, write_strength, level_weights, segment, out_gate, norm_gain, w_out):
    far = pl.BlockSpec(memory_space=pl.ANY)
    near = pl.BlockSpec(memory_space=pltpu.VMEM)
    tall = (HEADS_HERE, TOKENS_HERE, WIDTH)
    wide = (MESSAGE_ROWS, 2 * WIDTH)
    return pl.pallas_call(
        layer_kernel,
        out_shape=jax.ShapeDtypeStruct((256, 2048), BF16),
        in_specs=[far] * 10,
        out_specs=near,
        scratch_shapes=[
            pltpu.VMEM(tall, BF16),
            pltpu.VMEM(tall, BF16),
            pltpu.VMEM(tall, BF16),
            pltpu.VMEM(tall, BF16),
            pltpu.VMEM((4, 512, 2048), BF16),
            pltpu.VMEM((HEADS_HERE, TOKENS_HERE), F32),
            pltpu.VMEM((HEADS_HERE, TOKENS_HERE), F32),
            pltpu.VMEM((LEVELS, HEADS_HERE, TOKENS_HERE), F32),
            pltpu.VMEM((BLOCKS, BLOCK), jnp.int32),
            pltpu.VMEM((1, WIDTH), F32),
            pltpu.VMEM((BLOCKS, BLOCK, BLOCK), F32),
            pltpu.VMEM((7, BLOCK, BLOCK), BF16),
            pltpu.VMEM((2, HEADS_HERE, BLOCKS, BLOCK), F32),
            pltpu.VMEM((HEADS_HERE, BLOCK, BLOCK), F32),
            pltpu.VMEM(tall, BF16),
            pltpu.VMEM((HEADS_HERE, BLOCKS, BLOCK, BLOCK), F32),
            pltpu.VMEM((HEADS_HERE, BLOCKS, BLOCK, 2 * WIDTH), BF16),
            pltpu.VMEM((HEADS_HERE, 7, BLOCK, 2 * WIDTH), BF16),
            pltpu.VMEM((HEADS_HERE, 8, WIDTH), F32),
            pltpu.VMEM((HEADS_HERE, BLOCK, BLOCK), F32),
            pltpu.VMEM(tall, F32),
            pltpu.VMEM((HEADS_HERE, TOKENS_HERE, 6 * WIDTH), BF16),
            pltpu.VMEM(tall, F32),
            pltpu.VMEM(tall, BF16),
            pltpu.VMEM((256, 2048), BF16),
            pltpu.VMEM((256, 2048), F32),
            pltpu.VMEM((HEADS_HERE,) + wide, BF16),
            pltpu.VMEM((HEADS_HERE,) + wide, BF16),
            pltpu.VMEM((GROUPS, 4) + wide, BF16),
            pltpu.VMEM((GROUPS,) + wide, BF16),
            pltpu.VMEM((GROUPS, 8) + wide, BF16),
            pltpu.VMEM((HEADS_HERE, BLOCK, 2 * WIDTH), F32),
            pltpu.VMEM((HEADS_HERE, 8, 2 * WIDTH), F32),
            pltpu.VMEM((GROUPS, BLOCK, 2 * WIDTH), F32),
            pltpu.VMEM((GROUPS, 8, 2 * WIDTH), F32),
            pltpu.VMEM((HEADS_HERE, 5, BLOCK, WIDTH), BF16),
            pltpu.VMEM((BLOCKS, BLOCK), F32),
            pltpu.VMEM((BLOCKS, BLOCK), F32),
            pltpu.SemaphoreType.DMA((4, HEADS_HERE)),
            pltpu.SemaphoreType.DMA((5,)),
            pltpu.SemaphoreType.DMA,
            pltpu.SemaphoreType.DMA((2,)),
            pltpu.SemaphoreType.DMA((2, HEADS_HERE)),
            pltpu.SemaphoreType.DMA((2, GROUPS, 3)),
            pltpu.SemaphoreType.DMA((2, GROUPS, 7)),
            pltpu.SemaphoreType.DMA((2, GROUPS, 2)),
            pltpu.SemaphoreType.DMA((HEADS_HERE, 3)),
            pltpu.SemaphoreType.DMA((HEADS_HERE, 3)),
            pltpu.SemaphoreType.DMA((9,)),
            pltpu.SemaphoreType.DMA((9,)),
        ],
        compiler_params=pltpu.CompilerParams(
            collective_id=0, has_side_effects=True, vmem_limit_bytes=58 << 20
        ),
        cost_estimate=pl.CostEstimate(flops=24_000_000_000, bytes_accessed=16_000_000, transcendentals=0),
    )(
        queries,
        keys,
        values,
        out_gate,
        w_out,
        log_decay,
        write_strength,
        level_weights.transpose(1, 0, 2),
        segment.reshape(BLOCKS, BLOCK),
        norm_gain.reshape(1, WIDTH),
    )


def solution(mesh):
    placed = (
        P("ctx", "head"),
        P("ctx", "head"),
        P("ctx", "head"),
        P("head", "ctx"),
        P("head", "ctx"),
        P("head", None, "ctx"),
        P("ctx"),
        P("ctx", "head"),
        P(),
        P("head", None),
    )
    return jax.shard_map(
        shards, mesh=mesh, in_specs=placed, out_specs=P(("ctx", "head"), None), check_vma=False
    )
```

time: 70.2 us -> 67.3 us (0.959)
  the two profiles are of different devices: /device:TPU:8 before, /device:TPU:248 now
where the time goes in v2:
time: 67.3 us; the launch traced here: 67.2 us
  Pallas kernels  64.8 us (96%)
  local copies, waits for them, and re-layouts  2.3 us (3%)
    pallas_call x1, Pallas kernels, shards(): pl.pallas_call(layer_kernel, out_shape=jax.ShapeDtypeStruct((256, 2048),...  64.8 us
    unnamed x1, local copies, waits for them, and re-layouts  2.3 us

profile of v2, /device:TPU:248, one launch (start us, length us, event | category | flops | bytes accessed | tf_op | source)
XLA Modules:
  0.0 67.2 jit_solution(13242267407139890113)
XLA Ops:
  0.0 64.8 %shard_map.100 = bf16[256,2048]{1,0:T(8,128)(2,1)} custom-call(bf16[1024,512]{1,0:T(8,128)(2,1)} %q_hbm.1, bf16[1024,512]{1,0:T(8,128)(2,1)} %k_hbm.1, bf16[1024,512]{1,0:T(8,128)(2,1)} %v_hbm.1, bf16[1024,512]{1,0:T(8,128)(2,1)} %gate_hbm.1, bf16[512,2048]{1,0:T(8,128)(2,1)} %w_hbm.1, f32[4,1024]{1,0:T(4,128)} %decay_hbm.1, f32[4,1024]{1,0:T(4,128)} %strength_hbm.1, ...), custom_call_target="tpu_custom_call" | custom-call | flops 24000000000 | bytes 16000000 | tf_op jit(solution)/shard_map/pallas_call | solution.py:703
  64.8 2.3 %copy.12 = bf16[256,2048]{1,0:T(8,128)(2,1)} copy(bf16[256,2048]{1,0:T(8,128)(2,1)} %shard_map.100) | data formatting | bytes 2097152

commit v3 on v2

--- a/solution.py
+++ b/solution.py
@@ -196,23 +196,29 @@
 
 
 def joined(late, early):
-    keep_l, body_l = late
-    keep_e, body_e = early
+    keep_l, body_l, first_l, last_l = late
+    keep_e, body_e, first_e, last_e = early
+    same = (first_l == last_e).astype(F32)
     moved = dot(body_l[:, WIDTH:].astype(BF16), body_e.astype(BF16))
-    carried = jnp.concatenate([body_l[:, :WIDTH], keep_e[:, WIDTH:] * body_l[:, WIDTH:]], axis=1)
-    return keep_l * keep_e, keep_l * body_e + carried - moved
+    carried = jnp.concatenate([body_l[:, :WIDTH], (same * keep_e)[:, WIDTH:] * body_l[:, WIDTH:]], axis=1)
+    keep_l = same * keep_l
+    return keep_l * keep_e, keep_l * body_e + carried - same * moved, first_e, last_l
 
 
 def without_state(summary):
-    keep, body = summary
-    return keep, jnp.concatenate([jnp.zeros((BLOCK, WIDTH), F32), body[:, WIDTH:]], axis=1)
-
-
-def keep_rows(keep):
-    first, second, third = split3(keep)
-    return jnp.concatenate(
-        [first.astype(F32), second.astype(F32), third.astype(F32), jnp.zeros((13, 2 * WIDTH), F32)], axis=0
-    ).astype(BF16)
+    keep, body, first, last = summary
+    return keep, jnp.concatenate([jnp.zeros((BLOCK, WIDTH), F32), body[:, WIDTH:]], axis=1), first, last
+
+
+def chosen(use, one, other):
+    use = use.astype(F32)
+    return tuple(use * a + (1.0 - use) * b for a, b in zip(one, other))
+
+
+def tail_rows(summary):
+    keep, _, first_id, last_id = summary
+    parts = [part.astype(F32) for part in split3(keep)] + [first_id, last_id]
+    return jnp.concatenate(parts + [jnp.zeros((11, 2 * WIDTH), F32)], axis=0).astype(BF16)
 
 
 def layer_kernel(
@@ -256,22 +262,24 @@
     core_sent_ref,
     core_came_ref,
     quad_ref,
-    oct_sent_ref,
-    oct_ref,
+    half_sent_ref,
+    half_ref,
+    ring_sent_ref,
+    ring_ref,
     total_ref,
     keep_ref,
     prefix_ref,
     prekeep_ref,
     chip_ref,
     segs_ref,
-    before_ref,
     load_sem,
     small_sem,
     own_sem,
-    seg_sem,
     core_sem,
     quad_sem,
-    oct_sem,
+    half_sent_sem,
+    half_came_sem,
+    ring_sem,
     chip_sem,
     out_sem,
     in_sem,
@@ -285,10 +293,7 @@
     y = ctx // 16
     zq = lax.rem(z, 4)
     zh = z // 4
-    place = 2 * y + zh
-    count = lax.axis_size("ctx")
     right, left = lax.rem(x + 1, 4), lax.rem(x + 3, 4)
-    after, ahead = lax.rem(ctx + 1, count), lax.rem(ctx + count - 1, count)
     other_core = ctx + 1 - 2 * core
 
     def at(y_to, z_to):
@@ -297,11 +302,11 @@
     def quad_to(d):
         return at(y, zh * 4 + lax.rem(zq + d, 4))
 
-    def oct_to(d):
-        to = lax.rem(place + d, 8)
-        half = lax.rem(to, 2)
-        across = zh + half - 2 * zh * half
-        return at(to // 2, z + across * (7 - 2 * z))
+    def half_to(n):
+        return at(y, 7 - z + n * (2 * (zq // 3) - 1))
+
+    def ring_to(d):
+        return at(lax.rem(y + d, 4), z)
 
     def remote(source, target, sent, came, axis, to):
         return pltpu.make_async_remote_copy(
@@ -313,9 +318,9 @@
             device_id_type=MESH,
         )
 
-    partners = [("ctx", other_core), ("ctx", after), ("ctx", ahead)]
-    partners += [("ctx", quad_to(d)) for d in (1, 2, 3)]
-    partners += [("ctx", oct_to(d)) for d in range(1, 8)]
+    partners = [("ctx", other_core)]
+    partners += [("ctx", at(y, lax.rem(z + d, 8))) for d in range(1, 8)]
+    partners += [("ctx", ring_to(d)) for d in (1, 2, 3)]
     partners += [("head", lax.rem(x + d, 4)) for d in (1, 2, 3)]
 
     sources = ((k_hbm, k_ref), (v_hbm, v_ref), (q_hbm, q_ref), (gate_hbm, gate_ref))
@@ -358,7 +363,6 @@
         w_copy(6 + n, whole_ref.at[shard, half_rows], shard, half_rows, "ctx", other_core)
         for n, shard in enumerate((left, right, lax.rem(x + 2, 4)))
     ]
-    seg_copy = remote(segs_ref, before_ref, seg_sem.at[0], seg_sem.at[1], "ctx", after)
 
     def core_copy(head):
         return remote(
@@ -369,14 +373,24 @@
         mine = quad_ref.at[group, zq]
         return remote(mine, mine, quad_sem.at[0, group, d - 1], quad_sem.at[1, group, d - 1], "ctx", quad_to(d))
 
-    def oct_copy(group, d):
+    def half_copy(group, n):
         return remote(
-            oct_sent_ref.at[group],
-            oct_ref.at[group, place],
-            oct_sem.at[0, group, d - 1],
-            oct_sem.at[1, group, d - 1],
+            half_sent_ref.at[group],
+            half_ref.at[group],
+            half_sent_sem.at[group, n],
+            half_came_sem.at[group],
             "ctx",
-            oct_to(d),
+            half_to(n),
+        )
+
+    def ring_copy(group, d):
+        return remote(
+            ring_sent_ref.at[group],
+            ring_ref.at[group, y],
+            ring_sem.at[0, group, d - 1],
+            ring_sem.at[1, group, d - 1],
+            "ctx",
+            ring_to(d),
         )
 
     def chip_copy(group, part, head):
@@ -401,18 +415,18 @@
 
     def read(ref):
         tail = ref[BLOCK:, :].astype(F32)
-        return tail[0:1] + tail[1:2] + tail[2:3], ref[:BLOCK, :].astype(F32)
+        return tail[0:1] + tail[1:2] + tail[2:3], ref[:BLOCK, :].astype(F32), tail[3:4], tail[4:5]
 
     def write(ref, summary):
-        keep, body = summary
-        ref[:BLOCK, :] = body.astype(BF16)
-        ref[BLOCK:, :] = keep_rows(keep)
-
-    def flag_row():
-        same = (before_ref[7:8, WIDTH - 1 :] == segs_ref[0:1, :1]).astype(F32)
-        return jnp.broadcast_to(same, (1, WIDTH))
-
-    def summary_step(group, between):
+        ref[:BLOCK, :] = summary[1].astype(BF16)
+        ref[BLOCK:, :] = tail_rows(summary)
+
+    def own_ids():
+        first_id = jnp.broadcast_to(segs_ref[0:1, :1], (1, 2 * WIDTH))
+        last_id = jnp.broadcast_to(segs_ref[BLOCKS - 1 :, WIDTH - 1 :], (1, 2 * WIDTH))
+        return first_id, last_id
+
+    def summary_step(group, between, ready):
         heads = [2 * group, 2 * group + 1]
         for head in heads:
             for which in range(2):
@@ -433,22 +447,19 @@
             column_ref,
             between,
         )
-        if group == 0:
-            seg_copy.wait_recv()
-        flag = flag_row()
+        ready()
         for head, (body, keep) in zip(heads, found):
-            keep = jnp.concatenate([flag * keep, flag * keep], axis=1)
-            body = jnp.concatenate([body[:, :WIDTH], flag * body[:, WIDTH:]], axis=1)
+            keep = jnp.concatenate([keep, keep], axis=1)
             total_ref[head] = body
             keep_ref[head] = jnp.broadcast_to(keep, (8, 2 * WIDTH))
-            write(core_sent_ref.at[head], (keep, body))
+            write(core_sent_ref.at[head], (keep, body) + own_ids())
             core_copy(head).start()
 
     def chip_step(group):
         for head in (2 * group, 2 * group + 1):
             core_copy(head).wait_recv()
         head = own_head(group)
-        mine = keep_ref[head, 0:1, :], total_ref[head]
+        mine = (keep_ref[head, 0:1, :], total_ref[head]) + own_ids()
         other = read(core_came_ref.at[head])
         to = quad_ref.at[group, zq]
 
@@ -462,57 +473,85 @@
 
         for d in (1, 3, 2):
             quad_copy(group, d).start()
+
+    def store_prefix(group, prefix):
+        prefix_ref[group] = prefix[1]
+        prekeep_ref[group, 0:1, :] = prefix[0]
+        prekeep_ref[group, 1:2, :] = prefix[2]
+
+    def load_prefix(group):
+        first_id = prekeep_ref[group, 1:2, :]
+        return prekeep_ref[group, 0:1, :], prefix_ref[group], first_id, first_id
 
     def quad_step(group):
         for d in (1, 2, 3):
             quad_copy(group, d).wait_recv()
         parts = [read(quad_ref.at[group, n]) for n in range(4)]
         first, second = joined(parts[1], parts[0]), joined(parts[3], parts[2])
-        write(oct_sent_ref.at[group], joined(second, first))
-        for d in range(1, 8):
-
-            @pl.when(place + d < 8)
-            def _():
-                oct_copy(group, d).start()
+        write(half_sent_ref.at[group], joined(second, first))
+
+        @pl.when((zq == 0) | (zq == 3))
+        def _():
+            for n in (1, 0):
+                half_copy(group, n).start()
 
         head = own_head(group)
         odd = lax.rem(zq, 2)
         upper = zq // 2
-        keep, body = read(quad_ref.at[group, odd * (zq - odd)])
-        odd, upper = odd.astype(F32), upper.astype(F32)
-        keep, body = odd * keep + (1.0 - odd), odd * body
-        chip_ref[head, 0] = body[:, :WIDTH].astype(BF16)
-        before = without_state((keep, body))
-        over_keep, over = joined(before, first)
-        chip_ref[head, 1] = (upper * over[:, :WIDTH]).astype(BF16)
+        own_first = read(quad_ref.at[group, zq])[2]
+        none = jnp.ones((1, 2 * WIDTH), F32), jnp.zeros((BLOCK, 2 * WIDTH), F32), own_first, own_first
+        keep, body, first_id, last_id = read(quad_ref.at[group, odd * (zq - odd)])
+        same = (own_first == last_id).astype(F32)
+        near = chosen(odd, (same * keep, same * body, first_id, first_id), none)
+        chip_ref[head, 0] = near[1][:, :WIDTH].astype(BF16)
+        near = without_state(near)
+        far = chosen(upper, joined(near, first), near)
+        chip_ref[head, 1] = far[1][:, :WIDTH].astype(BF16)
         chip_copy(group, 0, head).start()
-        keep = upper * over_keep + (1.0 - upper) * before[0]
-        prekeep_ref[group] = jnp.broadcast_to(keep, (8, 2 * WIDTH))
-        prefix_ref[group] = upper * over + (1.0 - upper) * before[1]
-
-    def oct_step(group):
-        for d in range(1, 8):
-
-            @pl.when(place >= d)
+        store_prefix(group, without_state(far))
+
+    def ring_step(group):
+        half_copy(group, 0).wait_recv()
+        mine, other = read(half_sent_ref.at[group]), read(half_ref.at[group])
+
+        @pl.when(zh == 1)
+        def _():
+            write(ring_sent_ref.at[group], joined(mine, other))
+
+        @pl.when(zh == 0)
+        def _():
+            write(ring_sent_ref.at[group], joined(other, mine))
+
+        for d in (2, 1, 3):
+
+            @pl.when(y + d < 4)
             def _():
-                oct_copy(group, d).wait_recv()
+                ring_copy(group, d).start()
+
+        prefix = load_prefix(group)
+        over = chosen(zh, joined(prefix, other), prefix)
+        chip_ref[own_head(group), 2] = over[1][:, :WIDTH].astype(BF16)
+        store_prefix(group, without_state(over))
+
+    def last_step(group):
+        for d in range(1, 4):
+
+            @pl.when(y >= d)
+            def _():
+                ring_copy(group, d).wait_recv()
 
         head = own_head(group)
         odd, upper = lax.rem(y, 2), y // 2
 
         def slot(use, n):
-            return read(oct_ref.at[group, use * n + (1 - use) * 7])
-
-        prefix = without_state((prekeep_ref[group, 0:1, :], prefix_ref[group]))
-        sibling = joined(slot(odd, 2 * y - 1), slot(odd, 2 * y - 2))
-        pair = joined(slot(upper, 1), slot(upper, 0)), joined(slot(upper, 3), slot(upper, 2))
-        over = joined(prefix, slot(zh, place - 1))
-        oldest = joined(pair[1], pair[0])
-        chip_ref[head, 2] = over[1][:, :WIDTH].astype(BF16)
-        over = joined(without_state(over), sibling)
+            return read(ring_ref.at[group, use * n + (1 - use) * 3])
+
+        prefix = load_prefix(group)
+        oldest = joined(slot(upper, 1), slot(upper, 0))
+        over = chosen(odd, joined(prefix, slot(odd, y - 1)), prefix)
         chip_ref[head, 3] = over[1][:, :WIDTH].astype(BF16)
         over = joined(without_state(over), oldest)
-        chip_ref[head, 4] = over[1][:, :WIDTH].astype(BF16)
+        chip_ref[head, 4] = (upper.astype(F32) * over[1][:, :WIDTH]).astype(BF16)
         chip_copy(group, 1, head).start()
 
     def readout_step(head):
@@ -537,19 +576,18 @@
         silu_ref[head] = gate / (1.0 + jnp.exp(-gate)) * gain_ref[...]
 
     def own_states(head, first, last):
-        later = core.astype(F32)
-        keep, body = read(core_came_ref.at[head])
-        keep = later * keep[:, :WIDTH] + (1.0 - later)
-        erase = (later * body[:, WIDTH:]).astype(BF16)
+        keep, body, _, last_id = read(core_came_ref.at[head])
+        joins = core.astype(F32) * (own_ids()[0] == last_id).astype(F32)[:, :WIDTH]
+        keep = joins * keep[:, :WIDTH] + (1.0 - core.astype(F32))
+        erase = (joins * body[:, WIDTH:]).astype(BF16)
         states = [chip_ref[head, n] for n in range(first, last)]
         moved = dot(erase, jnp.concatenate(states, axis=1))
-        flag = flag_row()
         carried = [
-            (flag * (keep * state.astype(F32) - moved[:, n * WIDTH : (n + 1) * WIDTH])).astype(BF16)
+            (keep * state.astype(F32) - moved[:, n * WIDTH : (n + 1) * WIDTH]).astype(BF16)
             for n, state in enumerate(states)
         ]
         if first == 0:
-            carried = [(flag * later * body[:, :WIDTH]).astype(BF16)] + carried
+            carried = [(joins * body[:, :WIDTH]).astype(BF16)] + carried
         return jnp.concatenate(carried, axis=0)
 
     def await_states(group, part, head):
@@ -605,6 +643,11 @@
 
         lax.fori_loop(0, 8, tile, 0)
 
+    for group in range(GROUPS):
+        ring_ref[group, 3] = jnp.zeros((MESSAGE_ROWS, 2 * WIDTH), BF16)
+    barrier = pltpu.get_barrier_semaphore()
+    for axis, to in partners:
+        pl.semaphore_signal(barrier, inc=1, device_id={axis: to}, device_id_type=MESH)
     for copy in smalls[:3]:
         copy.start()
     for head in range(HEADS_HERE):
@@ -616,13 +659,6 @@
         for which in (2, 3):
             load(which, head).start()
     own_w.start()
-    for group in range(GROUPS):
-        for n in range(8):
-            oct_ref[group, n, :BLOCK, :] = jnp.zeros((BLOCK, 2 * WIDTH), BF16)
-            oct_ref[group, n, BLOCK:, :] = keep_rows(jnp.ones((1, 2 * WIDTH), F32))
-    barrier = pltpu.get_barrier_semaphore()
-    for axis, to in partners:
-        pl.semaphore_signal(barrier, inc=1, device_id={axis: to}, device_id_type=MESH)
     smalls[0].wait()
     segs_ref[...] = seg_ref[...].astype(F32)
     prepare_masks(seg_ref, far_ref, pair_ref)
@@ -631,52 +667,54 @@
         for each in range(HEADS_HERE):
             for b in range(BLOCKS):
                 spread_ref[n, each, b : b + 1, :] = source[each : each + 1, rows_of(b)]
-    pl.semaphore_wait(barrier, len(partners))
-    seg_copy.start()
+
+    def all_entered():
+        pl.semaphore_wait(barrier, len(partners))
+
+    summary_step(0, lambda: None, all_entered)
     for copy in w_first:
         copy.start()
-
-    summary_step(0, lambda: None)
-    summary_step(1, lambda: chip_step(0))
+    summary_step(1, lambda: chip_step(0), lambda: None)
     for copy in smalls[3:]:
         copy.wait()
+    gate_step(0)
+    chip_step(1)
+    quad_step(0)
     for level in range(10):
         for each in range(HEADS_HERE):
             for b in range(BLOCKS):
                 row = b * 16 + level
                 weight_ref[each, row : row + 1, :] = weights_ref[level, each : each + 1, rows_of(b)]
-    gate_step(0)
-    chip_step(1)
+    for head in range(HEADS_HERE):
+        readout_step(head)
+    gate_step(1)
+    quad_step(1)
     for n in range(2):
         w_first[n].wait_recv()
         w_relay[n].start()
-    readout_step(0)
-    quad_step(0)
-    for head in range(1, HEADS_HERE):
-        readout_step(head)
-    quad_step(1)
+    ring_step(0)
+    near_step(0, 0)
+    near_step(0, 1)
+    gate_step(2)
+    gate_step(3)
     for n in range(2):
         w_first[2 + n].wait_recv()
         w_core[n].start()
-    for head in range(1, HEADS_HERE):
-        gate_step(head)
-    near_step(0, 0)
-    near_step(0, 1)
-    oct_step(0)
     near_step(1, 2)
     near_step(1, 3)
+    ring_step(1)
+    last_step(0)
     finish_group(0)
     for copy in w_relay:
         copy.wait_recv()
     w_core[2].start()
-    oct_step(1)
+    last_step(1)
     finish_group(1)
     own_w.wait()
     for copy in w_core:
         copy.wait_recv()
     project_group(0)
     project_group(1)
-    seg_copy.wait_send()
     for copy in w_first + w_relay + w_core:
         copy.wait_send()
     for head in range(HEADS_HERE):
@@ -688,11 +726,16 @@
             quad_copy(group, d).wait_send()
         for part in range(2):
             chip_copy(group, part, own_head(group)).wait_send()
-        for d in range(1, 8):
-
-            @pl.when(place + d < 8)
+        for d in range(1, 4):
+
+            @pl.when(y + d < 4)
             def _():
-                oct_copy(group, d).wait_send()
+                ring_copy(group, d).wait_send()
+
+        @pl.when((zq == 0) | (zq == 3))
+        def _():
+            for n in range(2):
+                half_copy(group, n).wait_send()
 
 
 def shards(queries, keys, values, log_decay, write_strength, level_weights, segment, out_gate, norm_gain, w_out):
@@ -736,21 +779,23 @@
             pltpu.VMEM((HEADS_HERE,) + wide, BF16),
             pltpu.VMEM((GROUPS, 4) + wide, BF16),
             pltpu.VMEM((GROUPS,) + wide, BF16),
-            pltpu.VMEM((GROUPS, 8) + wide, BF16),
+            pltpu.VMEM((GROUPS,) + wide, BF16),
+            pltpu.VMEM((GROUPS,) + wide, BF16),
+            pltpu.VMEM((GROUPS, 4) + wide, BF16),
             pltpu.VMEM((HEADS_HERE, BLOCK, 2 * WIDTH), F32),
             pltpu.VMEM((HEADS_HERE, 8, 2 * WIDTH), F32),
             pltpu.VMEM((GROUPS, BLOCK, 2 * WIDTH), F32),
             pltpu.VMEM((GROUPS, 8, 2 * WIDTH), F32),
             pltpu.VMEM((HEADS_HERE, 5, BLOCK, WIDTH), BF16),
             pltpu.VMEM((BLOCKS, BLOCK), F32),
-            pltpu.VMEM((BLOCKS, BLOCK), F32),
             pltpu.SemaphoreType.DMA((4, HEADS_HERE)),
             pltpu.SemaphoreType.DMA((5,)),
             pltpu.SemaphoreType.DMA,
-            pltpu.SemaphoreType.DMA((2,)),
             pltpu.SemaphoreType.DMA((2, HEADS_HERE)),
             pltpu.SemaphoreType.DMA((2, GROUPS, 3)),
-            pltpu.SemaphoreType.DMA((2, GROUPS, 7)),
+            pltpu.SemaphoreType.DMA((GROUPS, 2)),
+            pltpu.SemaphoreType.DMA((GROUPS,)),
+            pltpu.SemaphoreType.DMA((2, GROUPS, 3)),
             pltpu.SemaphoreType.DMA((2, GROUPS, 2)),
             pltpu.SemaphoreType.DMA((HEADS_HERE, 3)),
             pltpu.SemaphoreType.DMA((HEADS_HERE, 3)),
@@ -758,7 +803,7 @@
             pltpu.SemaphoreType.DMA((9,)),
         ],
         compiler_params=pltpu.CompilerParams(
-            collective_id=0, has_side_effects=True, vmem_limit_bytes=58 << 20
+            collective_id=0, has_side_effects=True, vmem_limit_bytes=50 << 20
         ),
         cost_estimate=pl.CostEstimate(flops=24_000_000_000, bytes_accessed=16_000_000, transcendentals=0),
     )(

time: 67.3 us -> 67.2 us (level)
  the two profiles are of different devices: /device:TPU:248 before, /device:TPU:8 now
where the time goes in v3:
time: 67.2 us; the launch traced here: 66.7 us
  Pallas kernels  59.5 us (89%)
  local copies, waits for them, and re-layouts  7.12 us (11%)
    pallas_call x1, Pallas kernels, shards(): pl.pallas_call(layer_kernel, out_shape=jax.ShapeDtypeStruct((256, 2048),...  59.5 us
    unnamed x15, local copies, waits for them, and re-layouts  7.12 us

profile of v3, /device:TPU:8, one launch (start us, length us, event | category | flops | bytes accessed | tf_op | source)
XLA Modules:
  0.0 66.7 jit_solution(13928807519041942723)
XLA Ops:
  0.0 0.0 copy-start
  0.0 1.2 %copy-done = bf16[1024,512]{1,0:T(8,128)(2,1)S(1)} copy-done((bf16[1024,512]{1,0:T(8,128)(2,1)S(1)}, bf16[1024,512]{1,0:T(8,128)(2,1)}, u32[]{:S(2)}) %copy-start) | copy-done | bytes 1048600
  1.2 0.0 copy-start.1
  1.2 1.2 %copy-done.1 = bf16[1024,512]{1,0:T(8,128)(2,1)S(1)} copy-done((bf16[1024,512]{1,0:T(8,128)(2,1)S(1)}, bf16[1024,512]{1,0:T(8,128)(2,1)}, u32[]{:S(2)}) %copy-start.1) | copy-done | bytes 1048600
  2.5 0.0 copy-start.2
  2.5 0.9 %copy-done.2 = f32[4,12,1024]{2,0,1:T(4,128)S(1)} copy-done((f32[4,12,1024]{2,0,1:T(4,128)S(1)}, f32[4,12,1024]{2,0,1:T(4,128)}, u32[]{:S(2)}) %copy-start.2) | copy-done | bytes 196632
  3.4 0.0 copy-start.3
  3.4 0.7 %copy-done.3 = f32[4,1024]{1,0:T(4,128)S(1)} copy-done((f32[4,1024]{1,0:T(4,128)S(1)}, f32[4,1024]{1,0:T(4,128)}, u32[]{:S(2)}) %copy-start.3) | copy-done | bytes 16408
  4.1 0.0 copy-start.4
  4.1 0.7 %copy-done.4 = f32[4,1024]{1,0:T(4,128)S(1)} copy-done((f32[4,1024]{1,0:T(4,128)S(1)}, f32[4,1024]{1,0:T(4,128)}, u32[]{:S(2)}) %copy-start.4) | copy-done | bytes 16408
  4.8 0.0 copy-start.5
  4.8 0.7 %copy-done.5 = s32[1024]{0:T(1024)S(1)} copy-done((s32[1024]{0:T(1024)S(1)}, s32[1024]{0:T(1024)}, u32[]{:S(2)}) %copy-start.5) | copy-done | bytes 4120
  5.5 0.0 copy-start.6
  5.5 0.7 copy-done.6
  6.2 59.5 %shard_map.100 = bf16[256,2048]{1,0:T(8,128)(2,1)S(1)} custom-call(bf16[1024,512]{1,0:T(8,128)(2,1)S(1)} %copy-done, bf16[1024,512]{1,0:T(8,128)(2,1)S(1)} %copy-done.1, bf16[1024,512]{1,0:T(8,128)(2,1)} %v_hbm.1, bf16[1024,512]{1,0:T(8,128)(2,1)} %gate_hbm.1, bf16[512,2048]{1,0:T(8,128)(2,1)} %w_hbm.1, f32[4,1024]{1,0:T(4,128)S(1)} %copy-done.3, ...), custom_call_target="tpu_custom_call" | custom-call | flops 24000000000 | bytes 16000000 | tf_op jit(solution)/shard_map/pallas_call | solution.py:746
  65.7 1.0 %copy.12 = bf16[256,2048]{1,0:T(8,128)(2,1)} copy(bf16[256,2048]{1,0:T(8,128)(2,1)S(1)} %shard_map.100) | data formatting | bytes 2097152
Async XLA Ops:
  0.0 1.2 %copy-start = (bf16[1024,512]{1,0:T(8,128)(2,1)S(1)}, bf16[1024,512]{1,0:T(8,128)(2,1)}, u32[]{:S(2)}) copy-start(bf16[1024,512]{1,0:T(8,128)(2,1)} %q_hbm.1) | copy-start | bytes 3145732
  1.2 1.2 %copy-start.1 = (bf16[1024,512]{1,0:T(8,128)(2,1)S(1)}, bf16[1024,512]{1,0:T(8,128)(2,1)}, u32[]{:S(2)}) copy-start(bf16[1024,512]{1,0:T(8,128)(2,1)} %k_hbm.1) | copy-start | bytes 3145732
  2.5 0.9 %copy-start.2 = (f32[4,12,1024]{2,0,1:T(4,128)S(1)}, f32[4,12,1024]{2,0,1:T(4,128)}, u32[]{:S(2)}) copy-start(f32[4,12,1024]{2,0,1:T(4,128)} %param.15) | copy-start | bytes 589828
  3.4 0.7 %copy-start.3 = (f32[4,1024]{1,0:T(4,128)S(1)}, f32[4,1024]{1,0:T(4,128)}, u32[]{:S(2)}) copy-start(f32[4,1024]{1,0:T(4,128)} %decay_hbm.1) | copy-start | bytes 49156
  4.1 0.7 %copy-start.4 = (f32[4,1024]{1,0:T(4,128)S(1)}, f32[4,1024]{1,0:T(4,128)}, u32[]{:S(2)}) copy-start(f32[4,1024]{1,0:T(4,128)} %strength_hbm.1) | copy-start | bytes 49156
  4.8 0.7 %copy-start.5 = (s32[1024]{0:T(1024)S(1)}, s32[1024]{0:T(1024)}, u32[]{:S(2)}) copy-start(s32[1024]{0:T(1024)} %param.16) | copy-start | bytes 12292
  5.5 0.7 copy-start.6

commit v4 on v3

--- a/solution.py
+++ b/solution.py
@@ -668,15 +668,15 @@
             for b in range(BLOCKS):
                 spread_ref[n, each, b : b + 1, :] = source[each : each + 1, rows_of(b)]
 
-    def all_entered():
-        pl.semaphore_wait(barrier, len(partners))
-
-    summary_step(0, lambda: None, all_entered)
-    for copy in w_first:
+    pl.semaphore_wait(barrier, len(partners))
+    for copy in w_first[:2]:
         copy.start()
+    summary_step(0, lambda: None, lambda: None)
     summary_step(1, lambda: chip_step(0), lambda: None)
     for copy in smalls[3:]:
         copy.wait()
+    for copy in w_first[2:]:
+        copy.start()
     gate_step(0)
     chip_step(1)
     quad_step(0)
@@ -687,29 +687,29 @@
                 weight_ref[each, row : row + 1, :] = weights_ref[level, each : each + 1, rows_of(b)]
     for head in range(HEADS_HERE):
         readout_step(head)
-    gate_step(1)
-    quad_step(1)
     for n in range(2):
         w_first[n].wait_recv()
         w_relay[n].start()
+    gate_step(1)
+    quad_step(1)
     ring_step(0)
     near_step(0, 0)
     near_step(0, 1)
     gate_step(2)
     gate_step(3)
-    for n in range(2):
-        w_first[2 + n].wait_recv()
-        w_core[n].start()
     near_step(1, 2)
     near_step(1, 3)
     ring_step(1)
     last_step(0)
     finish_group(0)
+    for n in range(2):
+        w_first[2 + n].wait_recv()
+        w_core[n].start()
+    last_step(1)
+    finish_group(1)
     for copy in w_relay:
         copy.wait_recv()
     w_core[2].start()
-    last_step(1)
-    finish_group(1)
     own_w.wait()
     for copy in w_core:
         copy.wait_recv()
@@ -803,7 +803,7 @@
             pltpu.SemaphoreType.DMA((9,)),
         ],
         compiler_params=pltpu.CompilerParams(
-            collective_id=0, has_side_effects=True, vmem_limit_bytes=50 << 20
+            collective_id=0, has_side_effects=True, vmem_limit_bytes=58 << 20
         ),
         cost_estimate=pl.CostEstimate(flops=24_000_000_000, bytes_accessed=16_000_000, transcendentals=0),
     )(

time: 67.2 us -> 63.7 us (0.948)
  local copies, waits for them, and re-layouts: 7.12 us -> 2.3 us
  Pallas kernels: 59.5 us -> 61.3 us
    unnamed x15 -> x1, local copies, waits for them, and re-layouts: 7.12 us -> 2.3 us
    pallas_call x1, Pallas kernels: 59.5 us -> 61.3 us  [shards(): pl.pallas_call(layer_kernel, out_shape=jax.ShapeDtypeStruct((256, 2048),...]
where the time goes in v4:
time: 63.7 us; the launch traced here: 63.6 us
  Pallas kernels  61.3 us (96%)
  local copies, waits for them, and re-layouts  2.3 us (4%)
    pallas_call x1, Pallas kernels, shards(): pl.pallas_call(layer_kernel, out_shape=jax.ShapeDtypeStruct((256, 2048),...  61.3 us
    unnamed x1, local copies, waits for them, and re-layouts  2.3 us

profile of v4, /device:TPU:8, one launch (start us, length us, event | category | flops | bytes accessed | tf_op | source)
XLA Modules:
  0.0 63.6 jit_solution(18324507744303117827)
XLA Ops:
  0.0 61.3 %shard_map.100 = bf16[256,2048]{1,0:T(8,128)(2,1)} custom-call(bf16[1024,512]{1,0:T(8,128)(2,1)} %q_hbm.1, bf16[1024,512]{1,0:T(8,128)(2,1)} %k_hbm.1, bf16[1024,512]{1,0:T(8,128)(2,1)} %v_hbm.1, bf16[1024,512]{1,0:T(8,128)(2,1)} %gate_hbm.1, bf16[512,2048]{1,0:T(8,128)(2,1)} %w_hbm.1, f32[4,1024]{1,0:T(4,128)} %decay_hbm.1, f32[4,1024]{1,0:T(4,128)} %strength_hbm.1, ...), custom_call_target="tpu_custom_call" | custom-call | flops 24000000000 | bytes 16000000 | tf_op jit(solution)/shard_map/pallas_call | solution.py:746
  61.3 2.3 %copy.12 = bf16[256,2048]{1,0:T(8,128)(2,1)} copy(bf16[256,2048]{1,0:T(8,128)(2,1)} %shard_map.100) | data formatting | bytes 2097152

commit v5 on v4

--- a/solution.py
+++ b/solution.py
@@ -293,7 +293,7 @@
     y = ctx // 16
     zq = lax.rem(z, 4)
     zh = z // 4
-    right, left = lax.rem(x + 1, 4), lax.rem(x + 3, 4)
+    right, left, opposite = lax.rem(x + 1, 4), lax.rem(x + 3, 4), lax.rem(x + 2, 4)
     other_core = ctx + 1 - 2 * core
 
     def at(y_to, z_to):
@@ -344,6 +344,9 @@
     ]
     own_w = pltpu.make_async_copy(w_hbm, whole_ref.at[x], own_sem)
     quarters = [pl.ds(pl.multiple_of(core * 256 + part * 128, 128), 128) for part in range(2)]
+    pieces = [
+        pl.ds(pl.multiple_of(core * 256 + part * 128 + lax.rem(y, 2) * 64, 64), 64) for part in range(2)
+    ]
     half_rows = pl.ds(pl.multiple_of(core * 256, 256), 256)
 
     def w_copy(n, source, shard, rows, axis, to):
@@ -356,12 +359,16 @@
         w_copy(3, w_hbm.at[quarters[0]], x, quarters[0], "head", left),
     ]
     w_relay = [
-        w_copy(4, whole_ref.at[left, quarters[0]], left, quarters[0], "head", right),
-        w_copy(5, whole_ref.at[right, quarters[1]], right, quarters[1], "head", left),
+        w_copy(4, whole_ref.at[left, pieces[0]], left, pieces[0], "head", right),
+        w_copy(5, whole_ref.at[right, pieces[1]], right, pieces[1], "head", left),
+    ]
+    w_share = [
+        w_copy(9, whole_ref.at[opposite, pieces[0]], opposite, pieces[0], "ctx", at(y + 1 - 2 * lax.rem(y, 2), z)),
+        w_copy(10, whole_ref.at[opposite, pieces[1]], opposite, pieces[1], "ctx", at(3 - y, z)),
     ]
     w_core = [
         w_copy(6 + n, whole_ref.at[shard, half_rows], shard, half_rows, "ctx", other_core)
-        for n, shard in enumerate((left, right, lax.rem(x + 2, 4)))
+        for n, shard in enumerate((left, right, opposite))
     ]
 
     def core_copy(head):
@@ -623,25 +630,31 @@
             def _():
                 finish_step(group, 2 * group + 1 - turn)
 
-    def project_group(group):
+    def part_of(group, shard, columns):
+        mine = pl.ds(pl.multiple_of(shard * 512 + group * 256, 256), 256)
+        return dot(gathered_ref[:, mine], whole_ref[shard, group * 256 : (group + 1) * 256, columns])
+
+    def arrived(group, ways):
         for head in (2 * group, 2 * group + 1):
-            for d in (1, 2, 3):
+            for d in ways:
                 spread_copy(head, d).wait_recv()
 
+    def by_tiles(work):
         def tile(n, carry):
-            columns = pl.ds(pl.multiple_of(n * 256, 256), 256)
-            rows = slice(group * 256, (group + 1) * 256)
-            total = sum(
-                dot(gathered_ref[:, shard * 512 + group * 256 : shard * 512 + (group + 1) * 256], whole_ref[shard, rows, columns])
-                for shard in range(4)
-            )
-            if group == 0:
-                sum_ref[:, columns] = total
-            else:
-                result_ref[:, columns] = (total + sum_ref[:, columns]).astype(BF16)
+            work(pl.ds(pl.multiple_of(n * 512, 512), 512))
             return carry
 
-        lax.fori_loop(0, 8, tile, 0)
+        lax.fori_loop(0, 4, tile, 0)
+
+    def project_near(columns):
+        sum_ref[:, columns] = part_of(0, x, columns) + part_of(0, left, columns) + part_of(0, right, columns)
+
+    def project_far(columns):
+        sum_ref[:, columns] += part_of(0, opposite, columns)
+
+    def project_rest(columns):
+        total = sum(part_of(1, shard, columns) for shard in (x, left, right, opposite))
+        result_ref[:, columns] = (sum_ref[:, columns] + total).astype(BF16)
 
     for group in range(GROUPS):
         ring_ref[group, 3] = jnp.zeros((MESSAGE_ROWS, 2 * WIDTH), BF16)
@@ -700,6 +713,9 @@
     near_step(1, 2)
     near_step(1, 3)
     ring_step(1)
+    for n in range(2):
+        w_relay[n].wait_recv()
+        w_share[n].start()
     last_step(0)
     finish_group(0)
     for n in range(2):
@@ -707,15 +723,20 @@
         w_core[n].start()
     last_step(1)
     finish_group(1)
-    for copy in w_relay:
+    for copy in w_share:
         copy.wait_recv()
     w_core[2].start()
     own_w.wait()
-    for copy in w_core:
+    for copy in w_core[:2]:
         copy.wait_recv()
-    project_group(0)
-    project_group(1)
-    for copy in w_first + w_relay + w_core:
+    arrived(0, (1, 3))
+    by_tiles(project_near)
+    w_core[2].wait_recv()
+    arrived(0, (2,))
+    by_tiles(project_far)
+    arrived(1, (1, 3, 2))
+    by_tiles(project_rest)
+    for copy in w_first + w_relay + w_share + w_core:
         copy.wait_send()
     for head in range(HEADS_HERE):
         core_copy(head).wait_send()
@@ -799,8 +820,8 @@
             pltpu.SemaphoreType.DMA((2, GROUPS, 2)),
             pltpu.SemaphoreType.DMA((HEADS_HERE, 3)),
             pltpu.SemaphoreType.DMA((HEADS_HERE, 3)),
-            pltpu.SemaphoreType.DMA((9,)),
-            pltpu.SemaphoreType.DMA((9,)),
+            pltpu.SemaphoreType.DMA((11,)),
+            pltpu.SemaphoreType.DMA((11,)),
         ],
         compiler_params=pltpu.CompilerParams(
             collective_id=0, has_side_effects=True, vmem_limit_bytes=58 << 20

time: 63.7 us -> 59.6 us (0.936); the launches traced: 63.6 us -> 58.8 us
  Pallas kernels: 61.3 us -> 56.5 us
    pallas_call x1, Pallas kernels: 61.3 us -> 56.5 us  [shards(): pl.pallas_call(layer_kernel, out_shape=jax.ShapeDtypeStruct((256, 2048),...]
where the time goes in v5:
time: 59.6 us; the launch traced here: 58.8 us
  Pallas kernels  56.5 us (95%)
  local copies, waits for them, and re-layouts  2.3 us (4%)
    pallas_call x1, Pallas kernels, shards(): pl.pallas_call(layer_kernel, out_shape=jax.ShapeDtypeStruct((256, 2048),...  56.5 us
    unnamed x1, local copies, waits for them, and re-layouts  2.3 us

profile of v5, /device:TPU:8, one launch (start us, length us, event | category | flops | bytes accessed | tf_op | source)
XLA Modules:
  0.0 58.8 jit_solution(16058863499465309674)
XLA Ops:
  0.0 56.5 %shard_map.100 = bf16[256,2048]{1,0:T(8,128)(2,1)} custom-call(bf16[1024,512]{1,0:T(8,128)(2,1)} %q_hbm.1, bf16[1024,512]{1,0:T(8,128)(2,1)} %k_hbm.1, bf16[1024,512]{1,0:T(8,128)(2,1)} %v_hbm.1, bf16[1024,512]{1,0:T(8,128)(2,1)} %gate_hbm.1, bf16[512,2048]{1,0:T(8,128)(2,1)} %w_hbm.1, f32[4,1024]{1,0:T(4,128)} %decay_hbm.1, f32[4,1024]{1,0:T(4,128)} %strength_hbm.1, ...), custom_call_target="tpu_custom_call" | custom-call | flops 24000000000 | bytes 16000000 | tf_op jit(solution)/shard_map/pallas_call | solution.py:767
  56.5 2.3 %copy.12 = bf16[256,2048]{1,0:T(8,128)(2,1)} copy(bf16[256,2048]{1,0:T(8,128)(2,1)} %shard_map.100) | data formatting | bytes 2097152

commit v6 on v5

--- a/solution.py
+++ b/solution.py
@@ -681,10 +681,13 @@
             for b in range(BLOCKS):
                 spread_ref[n, each, b : b + 1, :] = source[each : each + 1, rows_of(b)]
 
-    pl.semaphore_wait(barrier, len(partners))
-    for copy in w_first[:2]:
-        copy.start()
-    summary_step(0, lambda: None, lambda: None)
+
+    def enter():
+        pl.semaphore_wait(barrier, len(partners))
+        for copy in w_first[:2]:
+            copy.start()
+
+    summary_step(0, enter, lambda: None)
     summary_step(1, lambda: chip_step(0), lambda: None)
     for copy in smalls[3:]:
         copy.wait()

time: 59.6 us -> 59.1 us (level)
  Pallas kernels: 56.5 us -> 55.9 us
where the time goes in v6:
time: 59.1 us; the launch traced here: 58.2 us
  Pallas kernels  55.9 us (95%)
  local copies, waits for them, and re-layouts  2.3 us (4%)
    pallas_call x1, Pallas kernels, shards(): pl.pallas_call(layer_kernel, out_shape=jax.ShapeDtypeStruct((256, 2048),...  55.9 us
    unnamed x1, local copies, waits for them, and re-layouts  2.3 us

profile of v6, /device:TPU:8, one launch (start us, length us, event | category | flops | bytes accessed | tf_op | source)
XLA Modules:
  0.0 58.2 jit_solution(15283342548760817459)
XLA Ops:
  0.0 55.9 %shard_map.100 = bf16[256,2048]{1,0:T(8,128)(2,1)} custom-call(bf16[1024,512]{1,0:T(8,128)(2,1)} %q_hbm.1, bf16[1024,512]{1,0:T(8,128)(2,1)} %k_hbm.1, bf16[1024,512]{1,0:T(8,128)(2,1)} %v_hbm.1, bf16[1024,512]{1,0:T(8,128)(2,1)} %gate_hbm.1, bf16[512,2048]{1,0:T(8,128)(2,1)} %w_hbm.1, f32[4,1024]{1,0:T(4,128)} %decay_hbm.1, f32[4,1024]{1,0:T(4,128)} %strength_hbm.1, ...), custom_call_target="tpu_custom_call" | custom-call | flops 24000000000 | bytes 16000000 | tf_op jit(solution)/shard_map/pallas_call | solution.py:770
  55.9 2.3 %copy.12 = bf16[256,2048]{1,0:T(8,128)(2,1)} copy(bf16[256,2048]{1,0:T(8,128)(2,1)} %shard_map.100) | data formatting | bytes 2097152
